TPU v7x, 256 devices: a whole 4x4x8 slice. The times are simulated.
256 devices in a mesh: sec: 4 (over z_hi, core), op: 64 (over z_lo, y, x).
Axes of the slice: x: 4, y: 4, z: 8 (z_hi: 2, z_lo: 4; z = z_hi * 4 + z_lo), core: 2. Of those that a mesh axis runs over, the one named last changes fastest.
Arguments:
- wave_in: float32 [4, 4, 256, 256], P('sec'), may hold values from -6 to 6
- kept_states: int32 [4, 4], P('sec'), may hold values from 64 to 256, as said below
- left_ops: bfloat16 [4, 512, 4, 256, 256], P('sec', 'op')
- right_ops: bfloat16 [4, 512, 4, 256, 256], P('sec', 'op'), may hold values from -0.375 to 0.375
Outputs:
- wave_out: float32 [4, 4, 256, 256], P('sec')
- boundary: float32 [4, 4, 256, 256], P('sec')
Inputs may be any that keep to these rules, and one draw needn't show every extreme that they name: `kept_states`: the first sector of every section keeps all 256 states.
All inputs are finite; a program needn't handle non-finite values.
Results may differ from a plain program's by a relative error of at most 0.0058.
Values sent between devices are 32-bit elements; how exact they have to be, the bound alone decides.
No kernel may reach another device: no remote copies, remote signals or barrier semaphores. Data moves between devices by JAX's collectives and lax.ppermute only.
A program may use at most 64 MiB of HBM per device.

v0:
```python
import math

import jax
import jax.numpy as jnp
from jax import lax
from jax.sharding import PartitionSpec as P

EPS = 1e-06
STEP_COEF = 0.5


def swapped(block, axis, apart):
    count = lax.axis_size(axis)
    route = []
    for low in range(count):
        high = low | 1 << apart
        if high != low and high < count:
            route += [(low, high), (high, low)]
    return lax.ppermute(block, axis, route)


def shifted(value, axis, steps):
    count = lax.axis_size(axis)
    pairs = [(source, (source + steps) % count) for source in range(count)]
    return lax.ppermute(value, axis, pairs)


def mixed_terms(state_b, right_ops):
    return jnp.einsum(
        "sij,ksjl->ksil", state_b, right_ops, preferred_element_type=jnp.float32
    ).astype(jnp.bfloat16)


def shards(wave_in, kept_states, left_ops, right_ops):
    sectors, width = (wave_in.shape[1], wave_in.shape[2])
    cols = jnp.arange(width, dtype=jnp.int32)
    mask = (cols[None, :] < kept_states[0][:, None]).astype(jnp.float32)[:, None, :]
    state = wave_in[0] * mask
    left = left_ops[0]
    right = right_ops[0]
    for step in range(2):
        mixed = mixed_terms(state.astype(jnp.bfloat16), right)
        partial_sigma = jnp.einsum(
            "ksij,ksjl->sil", left, mixed, preferred_element_type=jnp.float32
        )
        sigma = lax.psum(partial_sigma, "op")
        pp = jnp.sum(state * state)
        ps = jnp.sum(state * sigma)
        theta = ps / (pp + EPS)
        trial = mask * ((1.0 + STEP_COEF * theta) * state - STEP_COEF * sigma)
        state = trial * lax.rsqrt(jnp.mean(trial * trial) + EPS)
    even_state = swapped(state, "sec", 0)
    odd_state = shifted(state, "sec", 1)
    partner = even_state + odd_state
    bound = jnp.einsum("sji,sjl->sil", state, partner, precision=lax.Precision.HIGHEST) / math.sqrt(
        width
    )
    return (state[None], bound[None])


def solution(mesh):
    return jax.shard_map(
        shards,
        mesh=mesh,
        in_specs=(
            P("sec", None, None, None),
            P("sec", None),
            P("sec", "op", None, None, None),
            P("sec", "op", None, None, None),
        ),
        out_specs=(P("sec", None, None, None), P("sec", None, None, None)),
        check_vma=False,
    )
```

profile of v0, /device:TPU:0, one launch (start us, length us, event | category | flops | bytes accessed | tf_op | source)
XLA Modules:
  0.0 1493.0 jit_solution(15629786137134941594)
XLA Ops:
  7.2 0.0 all-reduce.3.cloned.1.call-start
  7.2 0.7 fusion.47
  7.9 1.6 copy.6
  9.5 7.0 fusion.20
  16.5 0.0 all-reduce.3.cloned.1.call-update
  16.5 0.0 all-reduce.5.cloned.1.call-start
  16.6 714.0 %all-reduce.3.cloned.1.call-done = f32[4,256,256]{1,2,0:T(8,128)} async-done(((f32[4,256,256]{1,2,0:T(8,128)}), f32[4,256,256]{1,2,0:T(8,128)}) %all-reduce.3.cloned.1.call-update) | async-done | bytes 1048592 | tf_op jit(solution)/shard_map/psum | solution.py:46
  730.6 2.2 multiply_reduce_fusion.4
  734.1 2.3 multiply_reduce_fusion.3
  737.0 6.8 fusion.27
  743.9 0.0 all-reduce.5.cloned.1.call-update
  743.9 715.2 %all-reduce.5.cloned.1.call-done = f32[4,256,256]{1,2,0:T(8,128)} async-done(((f32[4,256,256]{1,2,0:T(8,128)}), f32[4,256,256]{1,2,0:T(8,128)}) %all-reduce.5.cloned.1.call-update) | async-done | bytes 1048592 | tf_op jit(solution)/shard_map/psum | solution.py:46
  1459.1 0.0 copy-start
  1459.1 2.2 multiply_reduce_fusion.1
  1462.6 2.2 multiply_reduce_fusion
  1465.5 0.0 copy-done
  1465.5 0.2 broadcast_multiply_fusion
  1465.7 0.1 collective-permute-start
  1465.8 0.5 collective-permute-start.1
  1466.3 1.3 copy.10
  1467.6 0.8 collective-permute-done
  1468.5 15.6 %collective-permute-done.1 = f32[4,256,256]{1,2,0:T(8,128)S(1)} collective-permute-done((f32[4,256,256]{1,2,0:T(8,128)S(1)}, f32[4,256,256]{1,2,0:T(8,128)S(1)}, u32[]{:S(2)}, u32[]{:S(2)}) %collective-permute-start.1) | collective-permute-done | bytes 1048608 | tf_op jit(solution)/shard_map/ppermute | solution.py:25
  1484.0 2.2 fusion.34
Async XLA Ops:
  7.2 723.4 %all-reduce.3.cloned.1.call-start = ((), (), s32[]{:S(2)}) async-start(), calls=%async_computation | async-start | bytes 2097152 | tf_op jit(solution)/shard_map/psum | solution.py:46
  16.5 1442.5 %all-reduce.5.cloned.1.call-start = ((), (), s32[]{:S(2)}) async-start(), calls=%async_computation.1 | async-start | bytes 2097152 | tf_op jit(solution)/shard_map/psum | solution.py:46
  1459.1 6.4 copy-start
  1465.7 2.7 collective-permute-start
  1465.8 18.2 %collective-permute-start.1 = (f32[4,256,256]{1,2,0:T(8,128)S(1)}, f32[4,256,256]{1,2,0:T(8,128)S(1)}, u32[]{:S(2)}, u32[]{:S(2)}) collective-permute-start(f32[4,256,256]{1,2,0:T(8,128)S(1)} %broadcast_multiply_fusion), channel_id=1, source_target_pairs={{0,64},{64,128},{128,192},{192,0},{1,65},{65,129},{129,193},{193,1... | collective-permute-start | bytes 3145736 | tf_op jit(solution)/shard_map/ppermute | solution.py:25
Sparse Core Ops, SparseCore 0:
  16.7 713.8 all-reduce.2
  744.0 714.9 all-reduce.4
where the time goes:
time: 1490 us
  waiting for transfers between devices  1450 us (97%)
  between operations  18.1 us (1%)
  matrix products  16 us (1%)
    psum x2, waiting for transfers between devices, shards(): sigma = lax.psum(partial_sigma, 'op')  1430 us
  transfers between devices with their start and end apart: 4, of which 4 were waited for; matrix products, arithmetic and copies ran while one was open for 0% of the time, Pallas kernels for 0%

commit v1 on v0

v1 whole, which is shorter than its diff:
```python
import math

import jax
import jax.numpy as jnp
from jax import lax
from jax.sharding import Mesh, PartitionSpec as P

EPS = 1e-06
STEP_COEF = 0.5
SEC = ("zh", "core")
OP = ("z", "y", "x")
PLANE = ("y", "x")


def paired(value, axis, apart):
    count = lax.axis_size(axis)
    return lax.ppermute(value, axis, [(i, i ^ apart) for i in range(count)])


def summed(partial):
    rows, width = partial.shape
    ways = lax.axis_size(PLANE)
    piece = lax.all_to_all(partial.reshape(ways, rows // ways, width), PLANE, 0, 0).sum(0)
    near = paired(piece, "z", 1)
    far = paired(piece, "z", 2)
    corner = paired(piece, "z", 3)
    piece = (piece + near) + (far + corner)
    copies = jnp.broadcast_to(piece[None], (ways,) + piece.shape)
    return lax.all_to_all(copies, PLANE, 0, 0).reshape(rows, width)


def shards(wave_in, kept_states, left_ops, right_ops):
    sectors, width = (wave_in.shape[1], wave_in.shape[2])
    cols = jnp.arange(width, dtype=jnp.int32)
    mask = (cols[None, :] < kept_states[0][:, None]).astype(jnp.float32)[:, None, :]
    state = wave_in[0] * mask
    left = left_ops[0]
    right = right_ops[0]
    for step in range(2):
        mixed = jnp.einsum(
            "sij,ksjl->ksil", state.astype(jnp.bfloat16), right, preferred_element_type=jnp.float32
        ).astype(jnp.bfloat16)
        partial_sigma = jnp.einsum("ksij,ksjl->sil", left, mixed, preferred_element_type=jnp.float32)
        sigma = summed(partial_sigma.reshape(sectors * width, width)).reshape(state.shape)
        pp = jnp.sum(state * state)
        ps = jnp.sum(state * sigma)
        theta = ps / (pp + EPS)
        trial = mask * ((1.0 + STEP_COEF * theta) * state - STEP_COEF * sigma)
        state = trial * lax.rsqrt(jnp.mean(trial * trial) + EPS)
    even_state = lax.ppermute(state, "core", [(0, 1), (1, 0)])
    odd_state = lax.ppermute(state, SEC, [(i, (i + 1) % 4) for i in range(4)])
    partner = even_state + odd_state
    bound = jnp.einsum("sji,sjl->sil", state, partner, precision=lax.Precision.HIGHEST) / math.sqrt(width)
    return (state[None], bound[None])


def solution(mesh):
    split = Mesh(mesh.devices.reshape(2, 2, 4, 4, 4), SEC + OP)
    return jax.shard_map(
        shards,
        mesh=split,
        in_specs=(
            P(SEC, None, None, None),
            P(SEC, None),
            P(SEC, OP, None, None, None),
            P(SEC, OP, None, None, None),
        ),
        out_specs=(P(SEC, None, None, None), P(SEC, None, None, None)),
        check_vma=False,
    )
```

time: 1490 us -> 157 us (0.11)
  waiting for transfers between devices: 1450 us -> 63.2 us
  blocking collectives: 0 us -> 39.9 us
  starting transfers between devices: 0.67 us -> 19.7 us
    psum x2 -> x0, waiting for transfers between devices: 1430 us -> none  [shards(): sigma = lax.psum(partial_sigma, 'op')]
    all_to_all x0 -> x2, blocking collectives: none -> 39.9 us  [summed(): lax.all_to_all(partial.reshape(ways, rows // ways, width), PLANE, 0, 0)]
    all_to_all x0 -> x2, waiting for transfers between devices: none -> 26.9 us  [summed(): return lax.all_to_all(copies, PLANE, 0, 0).reshape(rows, width)]
    ppermute x2 -> x8, waiting for transfers between devices: 16.4 us -> 36.3 us  [the longest x1 26.4 us: shards(): odd_state = lax.ppermute(state, SEC, [(i, (i + 1) % 4) for i in range(4)])]
  transfers between devices with their start and end apart: 4 -> 10, of which waited for: 4 -> 8; matrix products, arithmetic and copies ran while one was open for 0% -> 3% of each run, Pallas kernels for 0% -> 0%
where the time goes in v1:
time: 157 us; the launch traced here: 156 us
  waiting for transfers between devices  63.2 us (40%)
  blocking collectives  39.9 us (25%)
  starting transfers between devices  19.7 us (13%)
  matrix products  15.8 us (10%)
  other arithmetic  10.5 us (7%)
  between operations  4.71 us (3%)
  local copies, waits for them, and re-layouts  2.17 us (1%)
    all_to_all x2, blocking collectives, summed(): lax.all_to_all(partial.reshape(ways, rows // ways, width), PLANE, 0, 0)  39.9 us
    all_to_all x2, waiting for transfers between devices, summed(): return lax.all_to_all(copies, PLANE, 0, 0).reshape(rows, width)  26.9 us
    ppermute x1, waiting for transfers between devices, shards(): odd_state = lax.ppermute(state, SEC, [(i, (i + 1) % 4) for i in range(4)])  26.4 us
    dot_general x2, matrix products, shards(): jnp.einsum('ksij,ksjl->sil', left, mixed, preferred_element_type=jnp.floa...  13 us
    ppermute x6, starting transfers between devices, paired(): return lax.ppermute(value, axis, [(i, i ^ apart) for i in range(count)])  11.1 us
    ppermute x6, waiting for transfers between devices, paired(): return lax.ppermute(value, axis, [(i, i ^ apart) for i in range(count)])  9.9 us
    all_to_all x2, starting transfers between devices, summed(): return lax.all_to_all(copies, PLANE, 0, 0).reshape(rows, width)  7.99 us
    reduce_sum x2, other arithmetic, shards(): ps = jnp.sum(state * sigma)  3.38 us
  transfers between devices with their start and end apart: 10, of which 8 were waited for; matrix products, arithmetic and copies ran while one was open for 3% of the time, Pallas kernels for 0%

profile of v1, /device:TPU:0, one launch (start us, length us, event | category | flops | bytes accessed | tf_op | source)
XLA Modules:
  0.0 155.9 jit_solution(1212509144225830802)
XLA Ops:
  0.6 0.7 fusion.35
  1.4 6.1 %fusion.2 = f32[4,256,256,1]{1,2,3,0:T(8,128)S(1)} fusion(f32[1,4,256,256]{3,2,1,0:T(8,128)} %param.4, f32[4,256]{1,0:T(4,128)S(1)} %fusion.35, bf16[1,8,4,256,256]{4,3,2,1,0:T(8,128)(2,1)} %param.6, bf16[1,8,4,256,256]{4,3,2,1,0:T(8,128)(2,1)} %param.7), kind=kOutput, calls=%fused_computation.2 | convolution fusion | flops 2150105088 | bytes 10489856 | tf_op jit(solution)/shard_map/ksij,ksjl->sil/dot_general | solution.py:43
  7.5 0.0 copy-start
  7.5 22.4 %all_to_all.20 = f32[16,64,256]{2,1,0:T(8,128)S(1)} all-to-all(f32[16,64,256]{2,1,0:T(8,128)S(1)} %bitcast.88), channel_id=1, replica_groups=mesh['zh'=2,'core'=2,'z'=4,'y'=4,'x'=4] {'y','x'}, dimensions={0} | all-to-all | bytes 2097152 | tf_op jit(solution)/shard_map/all_to_all | solution.py:23
  29.9 0.1 reduce_sum.72
  30.0 3.4 %collective-permute-start.1 = (f32[64,256]{1,0:T(8,128)S(1)}, f32[64,256]{1,0:T(8,128)S(1)}, u32[]{:S(2)}, u32[]{:S(2)}) collective-permute-start(f32[64,256]{1,0:T(8,128)S(1)} %reduce_sum.72), channel_id=1, source_target_pairs={{0,32},{16,48},{32,0},{48,16},{1,33},{17,49},{33,1},{49,17},{2,34}... | collective-permute-start | bytes 196616 | tf_op jit(solution)/shard_map/ppermute | solution.py:17
  33.3 1.5 collective-permute-start.2
  34.8 0.5 collective-permute-start
  35.2 0.4 collective-permute-done.1
  35.7 3.9 %collective-permute-done.2 = f32[64,256]{1,0:T(8,128)S(1)} collective-permute-done((f32[64,256]{1,0:T(8,128)S(1)}, f32[64,256]{1,0:T(8,128)S(1)}, u32[]{:S(2)}, u32[]{:S(2)}) %collective-permute-start.2) | collective-permute-done | bytes 65568 | tf_op jit(solution)/shard_map/ppermute | solution.py:17
  39.5 0.2 collective-permute-done
  39.8 1.1 broadcast_in_dim.6
  40.8 3.7 %all-to-all-start.1 = ((f32[16,64,256]{2,1,0:T(8,128)}), f32[16,64,256]{2,1,0:T(8,128)S(1)}, u32[]{:S(2)}, u32[]{:S(2)}) async-start(f32[16,64,256]{2,1,0:T(8,128)} %broadcast_in_dim.6), calls=%async_computation.1 | async-start | bytes 2097152 | tf_op jit(solution)/shard_map/all_to_all | solution.py:29
  44.5 0.0 copy-done
  44.5 0.9 multiply_reduce_fusion.4
  46.1 13.7 %all-to-all-done.1 = f32[16,64,256]{2,1,0:T(8,128)S(1)} async-done(((f32[16,64,256]{2,1,0:T(8,128)}), f32[16,64,256]{2,1,0:T(8,128)S(1)}, u32[]{:S(2)}, u32[]{:S(2)}) %all-to-all-start.1) | async-done | bytes 1048608 | tf_op jit(solution)/shard_map/all_to_all | solution.py:29
  59.8 0.0 copy-start.2
  59.8 0.9 multiply_reduce_fusion.5
  60.7 0.0 copy-start.1
  61.4 0.0 copy-done.2
  61.4 0.9 multiply_reduce_fusion.3
  63.0 6.8 %fusion = f32[4,256,256,1]{1,2,3,0:T(8,128)} fusion(f32[4,256,256]{2,1,0:T(8,128)S(1)} %get-tuple-element.3, f32[]{:T(128)S(6)} %rsqrt.6, bf16[1,8,4,256,256]{4,3,2,1,0:T(8,128)(2,1)} %param.6, bf16[1,8,4,256,256]{4,3,2,1,0:T(8,128)(2,1)} %param.7), kind=kOutput, calls=%fused_computation | convolution fusion | flops 2150105088 | bytes 10485764 | tf_op jit(solution)/shard_map/ksij,ksjl->sil/dot_general | solution.py:43
  69.8 0.0 copy-done.1
  69.8 17.5 %all_to_all.21 = f32[16,64,256]{2,1,0:T(8,128)S(1)} all-to-all(f32[16,64,256]{2,1,0:T(8,128)} %bitcast.89), channel_id=1, replica_groups=mesh['zh'=2,'core'=2,'z'=4,'y'=4,'x'=4] {'y','x'}, dimensions={0} | all-to-all | bytes 2097152 | tf_op jit(solution)/shard_map/all_to_all | solution.py:23
  87.3 0.1 reduce_sum.76
  87.4 5.1 %collective-permute-start.4 = (f32[64,256]{1,0:T(8,128)S(1)}, f32[64,256]{1,0:T(8,128)S(1)}, u32[]{:S(2)}, u32[]{:S(2)}) collective-permute-start(f32[64,256]{1,0:T(8,128)S(1)} %reduce_sum.76), channel_id=1, source_target_pairs={{0,32},{16,48},{32,0},{48,16},{1,33},{17,49},{33,1},{49,17},{2,34}... | collective-permute-start | bytes 196616 | tf_op jit(solution)/shard_map/ppermute | solution.py:17
  92.5 0.0 collective-permute-start.5
  92.5 0.7 collective-permute-start.3
  93.2 2.8 %collective-permute-done.4 = f32[64,256]{1,0:T(8,128)S(1)} collective-permute-done((f32[64,256]{1,0:T(8,128)S(1)}, f32[64,256]{1,0:T(8,128)S(1)}, u32[]{:S(2)}, u32[]{:S(2)}) %collective-permute-start.4) | collective-permute-done | bytes 65568 | tf_op jit(solution)/shard_map/ppermute | solution.py:17
  96.0 2.6 %collective-permute-done.5 = f32[64,256]{1,0:T(8,128)S(1)} collective-permute-done((f32[64,256]{1,0:T(8,128)S(1)}, f32[64,256]{1,0:T(8,128)S(1)}, u32[]{:S(2)}, u32[]{:S(2)}) %collective-permute-start.5) | collective-permute-done | bytes 65568 | tf_op jit(solution)/shard_map/ppermute | solution.py:17
  98.6 0.0 collective-permute-done.3
  98.6 1.1 broadcast_in_dim.7
  99.7 4.3 %all-to-all-start.3 = ((f32[16,64,256]{2,1,0:T(8,128)}), f32[16,64,256]{2,1,0:T(8,128)}, u32[]{:S(2)}, u32[]{:S(2)}) async-start(f32[16,64,256]{2,1,0:T(8,128)} %broadcast_in_dim.7), calls=%async_computation.3 | async-start | bytes 2097152 | tf_op jit(solution)/shard_map/all_to_all | solution.py:29
  104.0 0.9 multiply_reduce_fusion.1
  105.5 13.1 %all-to-all-done.3 = f32[16,64,256]{2,1,0:T(8,128)} async-done(((f32[16,64,256]{2,1,0:T(8,128)}), f32[16,64,256]{2,1,0:T(8,128)}, u32[]{:S(2)}, u32[]{:S(2)}) %all-to-all-start.3) | async-done | bytes 1048608 | tf_op jit(solution)/shard_map/all_to_all | solution.py:29
  118.7 2.5 %multiply_reduce_fusion.2 = (f32[]{:T(128)}, f32[16,64,256]{2,1,0:T(8,128)S(1)}) fusion(f32[16,64,256]{2,1,0:T(8,128)} %all-to-all-done.3, f32[16,64,256]{2,1,0:T(8,128)S(1)} %bitcast.82, f32[]{:T(128)S(6)} %rsqrt.6, f32[]{:T(128)S(6)} %add.43, f32[16,256]{1,0:T(8,128)S(1)} %mul.159, f32[16,64,256]{2,1,0:T(8,128)} %copy-done.2), kind=kLoop, calls=%fused_computation.23 | loop fusion | flops 2359295 | bytes 4210700 | tf_op jit(solution)/shard_map/reduce_sum | solution.py:46
  121.8 0.9 multiply_reduce_fusion
  123.4 0.2 broadcast_multiply_fusion
  123.6 0.1 collective-permute-start.6
  123.7 0.5 collective-permute-start.7
  124.1 2.5 %multiply_multiply_fusion = f32[1,4,256,256]{3,2,1,0:T(8,128)} fusion(f32[1,4,256,256]{3,2,1,0:T(8,128)S(1)} %bitcast.85, f32[1,4,256,256]{3,2,1,0:T(8,128)} %bitcast.87, f32[1,4,256,256]{3,2,1,0:T(8,128)S(1)} %copy-done, f32[]{:T(128)S(6)} %rsqrt.7, f32[]{:T(128)S(6)} %rsqrt.6, f32[]{:T(128)S(6)} %add.43, f32[]{:T(128)S(6)} %add.49, f32[4,256]{1,0:T(4,128)S(1)} %fusion.35), kind=kLoop, calls=%fused_computation.21 | loop fusion | flops 2359296 | bytes 4198416 | tf_op jit(solution)/shard_map/mul | solution.py:49
  126.7 0.0 collective-permute-done.6
  126.7 26.4 %collective-permute-done.7 = f32[4,256,256]{2,1,0:T(8,128)S(1)} collective-permute-done((f32[4,256,256]{2,1,0:T(8,128)S(1)}, f32[4,256,256]{2,1,0:T(8,128)S(1)}, u32[]{:S(2)}, u32[]{:S(2)}) %collective-permute-start.7) | collective-permute-done | bytes 1048608 | tf_op jit(solution)/shard_map/ppermute | solution.py:51
  153.1 2.8 %fusion.20 = f32[1,4,256,256]{3,2,1,0:T(8,128)} fusion(f32[4,256,256]{2,1,0:T(8,128)S(1)} %broadcast_multiply_fusion, f32[4,256,256]{2,1,0:T(8,128)S(1)} %collective-permute-done.6, f32[4,256,256]{2,1,0:T(8,128)S(1)} %collective-permute-done.7), kind=kOutput, calls=%fused_computation.13 | convolution fusion | flops 805830656 | bytes 4194304 | tf_op jit(solution)/shard_map/sji,sjl->sil/dot_general | solution.py:53
  (4 shorter events, 0.1 us)
Async XLA Ops:
  7.5 37.0 %copy-start = (f32[1,4,256,256]{3,2,1,0:T(8,128)S(1)}, f32[1,4,256,256]{3,2,1,0:T(8,128)}, u32[]{:S(2)}) copy-start(f32[1,4,256,256]{3,2,1,0:T(8,128)} %param.4) | copy-start | bytes 3145732
  30.0 5.7 %collective-permute-start.1 = (f32[64,256]{1,0:T(8,128)S(1)}, f32[64,256]{1,0:T(8,128)S(1)}, u32[]{:S(2)}, u32[]{:S(2)}) collective-permute-start(f32[64,256]{1,0:T(8,128)S(1)} %reduce_sum.72), channel_id=1, source_target_pairs={{0,32},{16,48},{32,0},{48,16},{1,33},{17,49},{33,1},{49,17},{2,34}... | collective-permute-start | bytes 196616 | tf_op jit(solution)/shard_map/ppermute | solution.py:17
  33.3 6.2 %collective-permute-start.2 = (f32[64,256]{1,0:T(8,128)S(1)}, f32[64,256]{1,0:T(8,128)S(1)}, u32[]{:S(2)}, u32[]{:S(2)}) collective-permute-start(f32[64,256]{1,0:T(8,128)S(1)} %reduce_sum.72), channel_id=1, source_target_pairs={{0,48},{16,32},{32,16},{48,0},{1,49},{17,33},{33,17},{49,1},{2,50}... | collective-permute-start | bytes 196616 | tf_op jit(solution)/shard_map/ppermute | solution.py:17
  34.8 5.0 %collective-permute-start = (f32[64,256]{1,0:T(8,128)S(1)}, f32[64,256]{1,0:T(8,128)S(1)}, u32[]{:S(2)}, u32[]{:S(2)}) collective-permute-start(f32[64,256]{1,0:T(8,128)S(1)} %reduce_sum.72), channel_id=1, source_target_pairs={{0,16},{16,0},{32,48},{48,32},{1,17},{17,1},{33,49},{49,33},{2,18}... | collective-permute-start | bytes 196616 | tf_op jit(solution)/shard_map/ppermute | solution.py:17
  40.8 19.0 %all-to-all-start.1 = ((f32[16,64,256]{2,1,0:T(8,128)}), f32[16,64,256]{2,1,0:T(8,128)S(1)}, u32[]{:S(2)}, u32[]{:S(2)}) async-start(f32[16,64,256]{2,1,0:T(8,128)} %broadcast_in_dim.6), calls=%async_computation.1 | async-start | bytes 2097152 | tf_op jit(solution)/shard_map/all_to_all | solution.py:29
  59.8 1.6 %copy-start.2 = (f32[16,64,256]{2,1,0:T(8,128)}, f32[16,64,256]{2,1,0:T(8,128)S(1)}, u32[]{:S(2)}) copy-start(f32[16,64,256]{2,1,0:T(8,128)S(1)} %all-to-all-done.1) | copy-start | bytes 3145732
  60.7 9.1 %copy-start.1 = (f32[16,64,256]{2,1,0:T(8,128)}, f32[16,64,256]{2,1,0:T(8,128)S(1)}, u32[]{:S(2)}) copy-start(f32[16,64,256]{2,1,0:T(8,128)S(1)} %get-tuple-element.7) | copy-start | bytes 3145732
  87.4 8.6 %collective-permute-start.4 = (f32[64,256]{1,0:T(8,128)S(1)}, f32[64,256]{1,0:T(8,128)S(1)}, u32[]{:S(2)}, u32[]{:S(2)}) collective-permute-start(f32[64,256]{1,0:T(8,128)S(1)} %reduce_sum.76), channel_id=1, source_target_pairs={{0,32},{16,48},{32,0},{48,16},{1,33},{17,49},{33,1},{49,17},{2,34}... | collective-permute-start | bytes 196616 | tf_op jit(solution)/shard_map/ppermute | solution.py:17
  92.5 6.1 %collective-permute-start.5 = (f32[64,256]{1,0:T(8,128)S(1)}, f32[64,256]{1,0:T(8,128)S(1)}, u32[]{:S(2)}, u32[]{:S(2)}) collective-permute-start(f32[64,256]{1,0:T(8,128)S(1)} %reduce_sum.76), channel_id=1, source_target_pairs={{0,48},{16,32},{32,16},{48,0},{1,49},{17,33},{33,17},{49,1},{2,50}... | collective-permute-start | bytes 196616 | tf_op jit(solution)/shard_map/ppermute | solution.py:17
  92.5 6.1 %collective-permute-start.3 = (f32[64,256]{1,0:T(8,128)S(1)}, f32[64,256]{1,0:T(8,128)S(1)}, u32[]{:S(2)}, u32[]{:S(2)}) collective-permute-start(f32[64,256]{1,0:T(8,128)S(1)} %reduce_sum.76), channel_id=1, source_target_pairs={{0,16},{16,0},{32,48},{48,32},{1,17},{17,1},{33,49},{49,33},{2,18}... | collective-permute-start | bytes 196616 | tf_op jit(solution)/shard_map/ppermute | solution.py:17
  99.7 19.0 %all-to-all-start.3 = ((f32[16,64,256]{2,1,0:T(8,128)}), f32[16,64,256]{2,1,0:T(8,128)}, u32[]{:S(2)}, u32[]{:S(2)}) async-start(f32[16,64,256]{2,1,0:T(8,128)} %broadcast_in_dim.7), calls=%async_computation.3 | async-start | bytes 2097152 | tf_op jit(solution)/shard_map/all_to_all | solution.py:29
  123.6 3.1 %collective-permute-start.6 = (f32[4,256,256]{2,1,0:T(8,128)S(1)}, f32[4,256,256]{2,1,0:T(8,128)S(1)}, u32[]{:S(2)}, u32[]{:S(2)}) collective-permute-start(f32[4,256,256]{2,1,0:T(8,128)S(1)} %broadcast_multiply_fusion), channel_id=1, source_target_pairs={{0,64},{64,0},{1,65},{65,1},{2,66},{66,2},{3,67},{67,3},{4,68},{68... | collective-permute-start | bytes 3145736 | tf_op jit(solution)/shard_map/ppermute | solution.py:50
  123.7 29.4 %collective-permute-start.7 = (f32[4,256,256]{2,1,0:T(8,128)S(1)}, f32[4,256,256]{2,1,0:T(8,128)S(1)}, u32[]{:S(2)}, u32[]{:S(2)}) collective-permute-start(f32[4,256,256]{2,1,0:T(8,128)S(1)} %broadcast_multiply_fusion), channel_id=1, source_target_pairs={{0,64},{64,128},{128,192},{192,0},{1,65},{65,129},{129,193},{193,1... | collective-permute-start | bytes 3145736 | tf_op jit(solution)/shard_map/ppermute | solution.py:51

commit v2 on v1

v2 whole, which is shorter than its diff:
```python
import functools
import math

import jax
import jax.numpy as jnp
from jax import lax
from jax.experimental import pallas as pl
from jax.experimental.pallas import tpu as pltpu
from jax.sharding import Mesh, PartitionSpec as P

EPS = 1e-06
STEP_COEF = 0.5
SEC = ("zh", "core")
OP = ("z1", "z0", "y", "x")
NEAR = ("z0", "y", "x")
SWAP = [(0, 1), (1, 0)]
VMEM_LIMIT = 24 * 2**20
CHUNK = 32


def mirrored():
    pairs = []
    for z in range(8):
        far = 7 - z
        pairs.append(((z // 4 * 2 + 1) * 4 + z % 4, (far // 4 * 2) * 4 + far % 4))
    return pairs


def masked(block, kept):
    cols = lax.broadcasted_iota(jnp.int32, block.shape, block.ndim - 1)
    return jnp.where(cols < kept, block, 0.0)


def folded(block):
    return block.reshape(-1, 8, block.shape[-1]).sum(0)


def chunk(i):
    return pl.ds(pl.multiple_of(i * CHUNK, CHUNK), CHUNK)


def update(rows, width, read_state, read_sigma, out_ref):
    count = rows // CHUNK
    zero = jnp.zeros((8, width), jnp.float32)

    def products(i, sums):
        state = read_state(i)
        return sums[0] + folded(state * state), sums[1] + folded(state * read_sigma(i))

    pp, ps = lax.fori_loop(0, count, products, (zero, zero), unroll=4)
    theta = jnp.sum(ps) / (jnp.sum(pp) + EPS)

    def trials(i, total):
        trial = (1.0 + STEP_COEF * theta) * read_state(i) - STEP_COEF * read_sigma(i)
        out_ref[chunk(i), :] = trial
        return total + folded(trial * trial)

    tt = lax.fori_loop(0, count, trials, zero, unroll=4)
    scale = lax.rsqrt(jnp.sum(tt) / (rows * width) + EPS)

    def scaled(i, carry):
        out_ref[chunk(i), :] = out_ref[chunk(i), :] * scale
        return carry

    lax.fori_loop(0, count, scaled, 0, unroll=4)


def sector_sums(state, left_ref, right_ref, s):
    terms = left_ref.shape[0]
    right = jnp.concatenate([right_ref[k, s] for k in range(terms)], axis=1)
    mixed = jnp.dot(state.astype(jnp.bfloat16), right, preferred_element_type=jnp.float32).astype(jnp.bfloat16)
    width = state.shape[1]
    mixed = jnp.concatenate([mixed[:, k * width : (k + 1) * width] for k in range(terms)], axis=0)
    left = jnp.concatenate([left_ref[k, s] for k in range(terms)], axis=1)
    return jnp.dot(left, mixed, preferred_element_type=jnp.float32)


def fetch(copies):
    started = []
    for s, (pairs, sems) in enumerate(copies):
        started.append([pltpu.make_async_copy(source, target, sems.at[j]) for j, (source, target) in enumerate(pairs)])
        for copy in started[s]:
            copy.start()
    return started


def first_kernel(kept_ref, wave_hbm, left_hbm, right_hbm, out_ref, left_ref, right_ref, wave_ref, sems):
    sectors, width = kept_ref.shape[1], wave_ref.shape[1]
    parts = [pl.ds(s * width, width) for s in range(sectors)]
    copies = fetch(
        [
            (
                [
                    (wave_hbm.at[parts[s]], wave_ref.at[parts[s]]),
                    (right_hbm.at[:, s], right_ref.at[:, s]),
                    (left_hbm.at[:, s], left_ref.at[:, s]),
                ],
                sems.at[s],
            )
            for s in range(sectors)
        ]
    )
    for s in range(sectors):
        for copy in copies[s]:
            copy.wait()
        out_ref[parts[s], :] = sector_sums(masked(wave_ref[parts[s], :], kept_ref[0, s]), left_ref, right_ref, s)


def second_kernel(kept_ref, wave_ref, sigma_ref, left_hbm, right_hbm, out_ref, state_ref, left_ref, right_ref, sems):
    sectors = kept_ref.shape[1]
    rows, width = wave_ref.shape
    share = rows // CHUNK // sectors
    copies = fetch(
        [
            (
                [(right_hbm.at[:, s], right_ref.at[:, s]), (left_hbm.at[:, s], left_ref.at[:, s])],
                sems.at[s],
            )
            for s in range(sectors)
        ]
    )
    update(
        rows,
        width,
        lambda i: masked(wave_ref[chunk(i), :], kept_ref[0, i // share]),
        lambda i: sigma_ref[chunk(i), :],
        state_ref,
    )
    for s in range(sectors):
        part = pl.ds(s * width, width)
        for copy in copies[s]:
            copy.wait()
        out_ref[part, :] = sector_sums(state_ref[part, :], left_ref, right_ref, s)


def own_kernel(state_ref, sigma_ref, out_ref):
    rows, width = state_ref.shape
    update(rows, width, lambda i: state_ref[chunk(i), :], lambda i: sigma_ref[chunk(i), :], out_ref)


def bound_kernel(sectors, core_ref, wave_ref, near_ref, far_ref, out_ref):
    width = wave_ref.shape[1]
    even = core_ref[0, 0] == 0
    for s in range(sectors):
        rows = pl.ds(s * width, width)
        near = near_ref[rows, :]
        partner = near + jnp.where(even, far_ref[rows, :], near)
        out_ref[rows, :] = lax.dot_general(
            wave_ref[rows, :],
            partner,
            (((0,), (0,)), ((), ())),
            precision=lax.Precision.HIGHEST,
            preferred_element_type=jnp.float32,
        ) / math.sqrt(width)


def params():
    return pltpu.CompilerParams(vmem_limit_bytes=VMEM_LIMIT)


def cost(flops, transfer):
    return pl.CostEstimate(flops=flops, bytes_accessed=transfer, transcendentals=0)


def smem():
    return pl.BlockSpec(memory_space=pltpu.SMEM)


def vmem():
    return pl.BlockSpec(memory_space=pltpu.VMEM)


def hbm():
    return pl.BlockSpec(memory_space=pltpu.HBM)


def in_hbm(*arrays):
    return [pltpu.with_memory_space_constraint(array, pltpu.HBM) for array in arrays]


def first_sums(kept, wave, left, right):
    terms, sectors, width, _ = left.shape
    return pl.pallas_call(
        first_kernel,
        in_specs=[smem()] + [hbm()] * 3,
        out_specs=vmem(),
        out_shape=jax.ShapeDtypeStruct(wave.shape, jnp.float32),
        scratch_shapes=[
            pltpu.VMEM(left.shape, left.dtype),
            pltpu.VMEM(right.shape, right.dtype),
            pltpu.VMEM(wave.shape, wave.dtype),
            pltpu.SemaphoreType.DMA((sectors, 3)),
        ],
        compiler_params=params(),
        cost_estimate=cost(4 * terms * sectors * width**3, 4 * left.size),
    )(kept, *in_hbm(wave, left, right))


def second_sums(kept, wave, sigma, left, right):
    terms, sectors, width, _ = left.shape
    return pl.pallas_call(
        second_kernel,
        in_specs=[smem()] + [vmem()] * 2 + [hbm()] * 2,
        out_specs=[vmem()] * 2,
        out_shape=[jax.ShapeDtypeStruct(wave.shape, jnp.float32)] * 2,
        scratch_shapes=[
            pltpu.VMEM(left.shape, left.dtype),
            pltpu.VMEM(right.shape, right.dtype),
            pltpu.SemaphoreType.DMA((sectors, 2)),
        ],
        compiler_params=params(),
        cost_estimate=cost(4 * terms * sectors * width**3, 4 * left.size),
    )(kept, wave, sigma, *in_hbm(left, right))


def gathered_sums(partial, kept):
    rows, width = partial.shape
    ways = lax.axis_size(NEAR)
    piece = lax.all_to_all(partial.reshape(ways, rows // ways, width), NEAR, 0, 0).sum(0)
    piece = piece + lax.ppermute(piece, "z1", SWAP)
    sector = lax.axis_index(NEAR) * kept.shape[1] // ways
    cols = jnp.arange(width, dtype=jnp.int32)
    piece = jnp.where(cols[None, :] < kept[0, sector], piece, 0.0)
    return lax.all_to_all(jnp.broadcast_to(piece[None], (ways,) + piece.shape), NEAR, 0, 0).reshape(rows, width)


def shards(wave_in, kept, left_ops, right_ops):
    _, sectors, width, _ = wave_in.shape
    core = lax.axis_index("core")
    wave = wave_in.reshape(sectors * width, width)
    like = jax.ShapeDtypeStruct(wave.shape, jnp.float32)

    left, right = left_ops[0], right_ops[0]
    sums = first_sums(kept, wave, left, right)
    sums, state = second_sums(kept, wave, gathered_sums(sums, kept), left, right)
    wave_out = pl.pallas_call(
        own_kernel,
        in_specs=[vmem()] * 2,
        out_specs=vmem(),
        out_shape=like,
        compiler_params=params(),
        cost_estimate=cost(12 * wave.size, 12 * wave.size),
    )(state, gathered_sums(sums, kept))
    far = lax.ppermute(wave_out, SEC + ("z1", "z0"), mirrored())
    near = lax.ppermute(wave_out, "core", SWAP)
    bound = pl.pallas_call(
        functools.partial(bound_kernel, sectors),
        in_specs=[smem()] + [vmem()] * 3,
        out_specs=vmem(),
        out_shape=like,
        compiler_params=params(),
        cost_estimate=cost(12 * sectors * width**3, 16 * wave.size),
    )(core.astype(jnp.int32).reshape(1, 1), wave_out, near, far)
    return (wave_out.reshape(wave_in.shape), bound.reshape(wave_in.shape))


def solution(mesh):
    split = Mesh(mesh.devices.reshape(2, 2, 2, 2, 4, 4), SEC + OP)
    return jax.shard_map(
        shards,
        mesh=split,
        in_specs=(
            P(SEC, None, None, None),
            P(SEC, None),
            P(SEC, OP, None, None, None),
            P(SEC, OP, None, None, None),
        ),
        out_specs=(P(SEC, None, None, None), P(SEC, None, None, None)),
        check_vma=False,
    )
```

time: 157 us -> 144 us (0.917)
  blocking collectives: 39.9 us -> 60.4 us
  waiting for transfers between devices: 63.2 us -> 44.6 us
  Pallas kernels: 0 us -> 16.5 us
  matrix products: 15.8 us -> 0 us
  other arithmetic: 10.5 us -> 0.8 us
  between operations: 4.71 us -> 0.74 us
  starting transfers between devices: 19.7 us -> 16.6 us
    all_to_all x2 -> x3, blocking collectives: 39.9 us -> 60.4 us  [the longest x2 40.1 us: gathered_sums(): lax.all_to_all(jnp.broadcast_to(piece[None], (ways,) + piece.shape), NEAR...]
    pallas_call x0 -> x4, Pallas kernels: none -> 16.5 us  [the longest x1 6.77 us: first_sums(): pl.pallas_call(first_kernel, in_specs=[smem()] + [hbm()] * 3, out_specs=v...]
    dot_general x3 -> x0, matrix products: 15.8 us -> none  [the longest x2 13 us: shards(): jnp.einsum('ksij,ksjl->sil', left, mixed, preferred_element_type=jnp.floa...]
    all_to_all x2 -> x1, waiting for transfers between devices: 26.9 us -> 15.9 us  [gathered_sums(): lax.all_to_all(partial.reshape(ways, rows // ways, width), NEAR, 0, 0)]
    ppermute x8 -> x4, waiting for transfers between devices: 36.3 us -> 28.7 us  [the longest x1 24.2 us: shards(): far = lax.ppermute(wave_out, SEC + ('z1', 'z0'), mirrored())]
    reduce_sum x8 -> x2, other arithmetic: 7.02 us -> 0.14 us  [gathered_sums(): lax.all_to_all(partial.reshape(ways, rows // ways, width), NEAR, 0, 0)]
    mul x2 -> x0, other arithmetic: 2.71 us -> none  [shards(): state = trial * lax.rsqrt(jnp.mean(trial * trial) + EPS)]
    ppermute x8 -> x4, starting transfers between devices: 11.7 us -> 9.54 us  [the longest x2 5 us: gathered_sums(): piece = piece + lax.ppermute(piece, 'z1', SWAP)]
  transfers between devices with their start and end apart: 10 -> 5, of which waited for: 8 -> 4; matrix products, arithmetic and copies ran while one was open for 3% -> 1% of each run, Pallas kernels for 0% -> 0%
where the time goes in v2:
time: 144 us; the launch traced here: 142 us
  blocking collectives  60.4 us (42%)
  waiting for transfers between devices  44.6 us (31%)
  starting transfers between devices  16.6 us (12%)
  Pallas kernels  16.5 us (11%)
  local copies, waits for them, and re-layouts  2.69 us (2%)
    all_to_all x2, blocking collectives, gathered_sums(): lax.all_to_all(jnp.broadcast_to(piece[None], (ways,) + piece.shape), NEAR...  40.1 us
    ppermute x1, waiting for transfers between devices, shards(): far = lax.ppermute(wave_out, SEC + ('z1', 'z0'), mirrored())  24.2 us
    all_to_all x1, blocking collectives, gathered_sums(): lax.all_to_all(partial.reshape(ways, rows // ways, width), NEAR, 0, 0)  20.4 us
    all_to_all x1, waiting for transfers between devices, gathered_sums(): lax.all_to_all(partial.reshape(ways, rows // ways, width), NEAR, 0, 0)  15.9 us
    all_to_all x1, starting transfers between devices, gathered_sums(): lax.all_to_all(partial.reshape(ways, rows // ways, width), NEAR, 0, 0)  7.08 us
    pallas_call x1, Pallas kernels, first_sums(): pl.pallas_call(first_kernel, in_specs=[smem()] + [hbm()] * 3, out_specs=v...  6.77 us
    pallas_call x1, Pallas kernels, second_sums(): pl.pallas_call(second_kernel, in_specs=[smem()] + [vmem()] * 2 + [hbm()]...  5.67 us
    ppermute x2, starting transfers between devices, gathered_sums(): piece = piece + lax.ppermute(piece, 'z1', SWAP)  5 us
  transfers between devices with their start and end apart: 5, of which 4 were waited for; matrix products, arithmetic and copies ran while one was open for 1% of the time, Pallas kernels for 0%

profile of v2, /device:TPU:0, one launch (start us, length us, event | category | flops | bytes accessed | tf_op | source)
XLA Modules:
  0.0 142.3 jit_solution(5697591280356142766)
XLA Ops:
  0.6 0.0 copy-start.2
  0.6 0.6 copy-done.2
  1.3 0.0 copy-start.3
  1.3 6.8 %shard_map.59 = f32[1024,256]{1,0:T(8,128)} custom-call(s32[1,4]{1,0:T(1,128)S(1)} %copy-done.2, f32[1024,256]{1,0:T(8,128)} %bitcast.14, bf16[8,4,256,256]{3,2,1,0:T(8,128)(2,1)} %bitcast.17, bf16[8,4,256,256]{3,2,1,0:T(8,128)(2,1)} %bitcast.19), custom_call_target="tpu_custom_call" | custom-call | flops 2147483648 | bytes 8388608 | tf_op jit(solution)/shard_map/pallas_call | solution.py:183
  8.1 0.0 copy-start.1
  8.1 7.1 %all-to-all-start = ((f32[32,32,256]{2,1,0:T(8,128)}), f32[32,32,256]{2,1,0:T(8,128)S(1)}, u32[]{:S(2)}, u32[]{:S(2)}) async-start(f32[32,32,256]{2,1,0:T(8,128)} %bitcast.4), calls=%async_computation | async-start | bytes 2097152 | tf_op jit(solution)/shard_map/all_to_all | solution.py:219
  15.2 0.0 copy-done.3
  15.2 0.6 constant_dynamic-slice_fusion
  15.8 15.9 %all-to-all-done = f32[32,32,256]{2,1,0:T(8,128)S(1)} async-done(((f32[32,32,256]{2,1,0:T(8,128)}), f32[32,32,256]{2,1,0:T(8,128)S(1)}, u32[]{:S(2)}, u32[]{:S(2)}) %all-to-all-start) | async-done | bytes 1048608 | tf_op jit(solution)/shard_map/all_to_all | solution.py:219
  31.7 0.1 reduce_sum.18
  31.8 3.4 %collective-permute-start = (f32[32,256]{1,0:T(8,128)S(1)}, f32[32,256]{1,0:T(8,128)S(1)}, u32[]{:S(2)}, u32[]{:S(2)}) collective-permute-start(f32[32,256]{1,0:T(8,128)S(1)} %reduce_sum.18), channel_id=1, source_target_pairs={{0,32},{32,0},{1,33},{33,1},{2,34},{34,2},{3,35},{35,3},{4,36},{36... | collective-permute-start | bytes 98312 | tf_op jit(solution)/shard_map/ppermute | solution.py:220
  35.1 0.6 iota_compare_fusion
  35.8 1.2 collective-permute-done
  37.0 0.1 broadcast_in_dim.32
  37.1 20.8 %all_to_all.20 = f32[32,32,256]{2,1,0:T(8,128)S(1)} all-to-all(f32[32,32,256]{2,1,0:T(8,128)S(1)} %broadcast_in_dim.32), channel_id=1, replica_groups=mesh['zh'=2,'core'=2,'z1'=2,'z0'=2,'y'=4,'x'=4] {'z0','y','x'}, dimensions={0} | all-to-all | bytes 2097152 | tf_op jit(solution)/shard_map/all_to_all | solution.py:224
  58.0 0.0 copy-done.1
  58.0 5.7 %shard_map.60 = (f32[1024,256]{1,0:T(8,128)S(1)}, f32[1024,256]{1,0:T(8,128)S(1)}) custom-call(s32[1,4]{1,0:T(1,128)S(1)} %copy-done.3, f32[1024,256]{1,0:T(8,128)S(1)} %bitcast.15, f32[1024,256]{1,0:T(8,128)S(1)} %bitcast.13, bf16[8,4,256,256]{3,2,1,0:T(8,128)(2,1)} %bitcast.18, bf16[8,4,256,256]{3,2,1,0:T(8,128)(2,1)} %bitcast.20), custom_call_target="tpu_custom_call" | custom-call | flops 2147483648 | bytes 8388608 | tf_op jit(solution)/shard_map/pallas_call | solution.py:201
  63.6 20.4 %all_to_all.21 = f32[32,32,256]{2,1,0:T(8,128)S(1)} all-to-all(f32[32,32,256]{2,1,0:T(8,128)S(1)} %bitcast.16), channel_id=1, replica_groups=mesh['zh'=2,'core'=2,'z1'=2,'z0'=2,'y'=4,'x'=4] {'z0','y','x'}, dimensions={0} | all-to-all | bytes 2097152 | tf_op jit(solution)/shard_map/all_to_all | solution.py:219
  84.0 0.1 reduce_sum.19
  84.1 1.6 %collective-permute-start.1 = (f32[32,256]{1,0:T(8,128)S(1)}, f32[32,256]{1,0:T(8,128)S(1)}, u32[]{:S(2)}, u32[]{:S(2)}) collective-permute-start(f32[32,256]{1,0:T(8,128)S(1)} %reduce_sum.19), channel_id=1, source_target_pairs={{0,32},{32,0},{1,33},{33,1},{2,34},{34,2},{3,35},{35,3},{4,36},{36... | collective-permute-start | bytes 98312 | tf_op jit(solution)/shard_map/ppermute | solution.py:220
  85.7 3.3 %collective-permute-done.1 = f32[32,256]{1,0:T(8,128)S(1)} collective-permute-done((f32[32,256]{1,0:T(8,128)S(1)}, f32[32,256]{1,0:T(8,128)S(1)}, u32[]{:S(2)}, u32[]{:S(2)}) %collective-permute-start.1) | collective-permute-done | bytes 32800 | tf_op jit(solution)/shard_map/ppermute | solution.py:220
  89.0 0.1 broadcast_in_dim.33
  89.1 19.3 %all_to_all.22 = f32[32,32,256]{2,1,0:T(8,128)S(1)} all-to-all(f32[32,32,256]{2,1,0:T(8,128)S(1)} %broadcast_in_dim.33), channel_id=1, replica_groups=mesh['zh'=2,'core'=2,'z1'=2,'z0'=2,'y'=4,'x'=4] {'z0','y','x'}, dimensions={0} | all-to-all | bytes 2097152 | tf_op jit(solution)/shard_map/all_to_all | solution.py:224
  108.3 1.8 %shard_map.61.wave_ref = f32[1024,256]{1,0:T(8,128)} custom-call(f32[1024,256]{1,0:T(8,128)S(1)} %get-tuple-element.4.state_ref, f32[1024,256]{1,0:T(8,128)S(1)} %bitcast.12), custom_call_target="tpu_custom_call" | custom-call | flops 3145728 | bytes 3145728 | tf_op jit(solution)/shard_map/pallas_call | solution.py:236
  110.2 1.3 collective-permute-start.3
  111.5 3.3 %collective-permute-start.2 = (f32[1024,256]{1,0:T(8,128)}, f32[1024,256]{1,0:T(8,128)S(1)}, u32[]{:S(2)}, u32[]{:S(2)}) collective-permute-start(f32[1024,256]{1,0:T(8,128)} %shard_map.61.wave_ref), channel_id=1, source_target_pairs={{0,64},{64,0},{1,65},{65,1},{2,66},{66,2},{3,67},{67,3},{4,68},{68... | collective-permute-start | bytes 3145736 | tf_op jit(solution)/shard_map/ppermute | solution.py:245
  114.7 24.2 %collective-permute-done.3.far_ref = f32[1024,256]{1,0:T(8,128)S(1)} collective-permute-done((f32[1024,256]{1,0:T(8,128)}, f32[1024,256]{1,0:T(8,128)S(1)}, u32[]{:S(2)}, u32[]{:S(2)}) %collective-permute-start.3) | collective-permute-done | bytes 1048608 | tf_op jit(solution)/shard_map/ppermute | solution.py:244
  138.9 0.0 collective-permute-done.2.near_ref
  138.9 0.0 copy-start
  138.9 1.2 copy-done
  140.2 2.2 %shard_map.62 = f32[1024,256]{1,0:T(8,128)} custom-call(s32[1,1]{1,0:T(1,128)} %bitcast.9.core_ref, f32[1024,256]{1,0:T(8,128)S(1)} %copy-done, f32[1024,256]{1,0:T(8,128)S(1)} %collective-permute-done.2.near_ref, f32[1024,256]{1,0:T(8,128)S(1)} %collective-permute-done.3.far_ref), custom_call_target="tpu_custom_call" | custom-call | flops 805306368 | bytes 4194304 | tf_op jit(solution)/shard_map/pallas_call | solution.py:246
  (2 shorter events, 0.0 us)
Async XLA Ops:
  0.6 0.7 copy-start.2
  1.3 13.9 %copy-start.3 = (s32[1,4]{1,0:T(1,128)S(1)}, s32[1,4]{1,0:T(1,128)}, u32[]{:S(2)}) copy-start(s32[1,4]{1,0:T(1,128)} %kept_ref.3) | copy-start | bytes 52
  8.1 49.9 %copy-start.1 = (f32[1,4,256,256]{3,2,1,0:T(8,128)S(1)}, f32[1,4,256,256]{3,2,1,0:T(8,128)}, u32[]{:S(2)}) copy-start(f32[1,4,256,256]{3,2,1,0:T(8,128)} %param.4) | copy-start | bytes 3145732
  8.1 23.6 %all-to-all-start = ((f32[32,32,256]{2,1,0:T(8,128)}), f32[32,32,256]{2,1,0:T(8,128)S(1)}, u32[]{:S(2)}, u32[]{:S(2)}) async-start(f32[32,32,256]{2,1,0:T(8,128)} %bitcast.4), calls=%async_computation | async-start | bytes 2097152 | tf_op jit(solution)/shard_map/all_to_all | solution.py:219
  31.8 5.3 %collective-permute-start = (f32[32,256]{1,0:T(8,128)S(1)}, f32[32,256]{1,0:T(8,128)S(1)}, u32[]{:S(2)}, u32[]{:S(2)}) collective-permute-start(f32[32,256]{1,0:T(8,128)S(1)} %reduce_sum.18), channel_id=1, source_target_pairs={{0,32},{32,0},{1,33},{33,1},{2,34},{34,2},{3,35},{35,3},{4,36},{36... | collective-permute-start | bytes 98312 | tf_op jit(solution)/shard_map/ppermute | solution.py:220
  84.1 4.9 %collective-permute-start.1 = (f32[32,256]{1,0:T(8,128)S(1)}, f32[32,256]{1,0:T(8,128)S(1)}, u32[]{:S(2)}, u32[]{:S(2)}) collective-permute-start(f32[32,256]{1,0:T(8,128)S(1)} %reduce_sum.19), channel_id=1, source_target_pairs={{0,32},{32,0},{1,33},{33,1},{2,34},{34,2},{3,35},{35,3},{4,36},{36... | collective-permute-start | bytes 98312 | tf_op jit(solution)/shard_map/ppermute | solution.py:220
  110.2 28.8 %collective-permute-start.3 = (f32[1024,256]{1,0:T(8,128)}, f32[1024,256]{1,0:T(8,128)S(1)}, u32[]{:S(2)}, u32[]{:S(2)}) collective-permute-start(f32[1024,256]{1,0:T(8,128)} %shard_map.61.wave_ref), channel_id=1, source_target_pairs={{64,176},{80,160},{96,144},{112,128},{192,48},{208,32},{224,16},{2... | collective-permute-start | bytes 3145736 | tf_op jit(solution)/shard_map/ppermute | solution.py:244
  111.5 27.5 %collective-permute-start.2 = (f32[1024,256]{1,0:T(8,128)}, f32[1024,256]{1,0:T(8,128)S(1)}, u32[]{:S(2)}, u32[]{:S(2)}) collective-permute-start(f32[1024,256]{1,0:T(8,128)} %shard_map.61.wave_ref), channel_id=1, source_target_pairs={{0,64},{64,0},{1,65},{65,1},{2,66},{66,2},{3,67},{67,3},{4,68},{68... | collective-permute-start | bytes 3145736 | tf_op jit(solution)/shard_map/ppermute | solution.py:245
  138.9 1.2 copy-start

commit v3 on v2

--- a/solution.py
+++ b/solution.py
@@ -1,4 +1,3 @@
-import functools
 import math
 
 import jax
@@ -138,20 +137,30 @@
     update(rows, width, lambda i: state_ref[chunk(i), :], lambda i: sigma_ref[chunk(i), :], out_ref)
 
 
-def bound_kernel(sectors, core_ref, wave_ref, near_ref, far_ref, out_ref):
+def bound_kernel(place_ref, wave_ref, near_ref, *refs):
+    sectors = len(refs) - 4
+    far_refs, (wave_out, bound_out, bound_ref, sems) = refs[:sectors], refs[sectors:]
     width = wave_ref.shape[1]
-    even = core_ref[0, 0] == 0
-    for s in range(sectors):
-        rows = pl.ds(s * width, width)
+    leaving = pltpu.make_async_copy(wave_ref, wave_out, sems.at[sectors])
+    leaving.start()
+    even = place_ref[0, 0] == 0
+    copies = []
+    for k in range(sectors):
+        rows = pl.ds(pl.multiple_of((place_ref[0, 1] ^ k) * width, width), width)
         near = near_ref[rows, :]
-        partner = near + jnp.where(even, far_ref[rows, :], near)
-        out_ref[rows, :] = lax.dot_general(
+        partner = near + jnp.where(even, far_refs[k][...], near)
+        bound_ref[rows, :] = lax.dot_general(
             wave_ref[rows, :],
             partner,
             (((0,), (0,)), ((), ())),
             precision=lax.Precision.HIGHEST,
             preferred_element_type=jnp.float32,
         ) / math.sqrt(width)
+        copies.append(pltpu.make_async_copy(bound_ref.at[rows], bound_out.at[rows], sems.at[k]))
+        copies[k].start()
+    for copy in copies:
+        copy.wait()
+    leaving.wait()
 
 
 def params():
@@ -226,7 +235,6 @@
 
 def shards(wave_in, kept, left_ops, right_ops):
     _, sectors, width, _ = wave_in.shape
-    core = lax.axis_index("core")
     wave = wave_in.reshape(sectors * width, width)
     like = jax.ShapeDtypeStruct(wave.shape, jnp.float32)
 
@@ -241,16 +249,21 @@
         compiler_params=params(),
         cost_estimate=cost(12 * wave.size, 12 * wave.size),
     )(state, gathered_sums(sums, kept))
-    far = lax.ppermute(wave_out, SEC + ("z1", "z0"), mirrored())
     near = lax.ppermute(wave_out, "core", SWAP)
-    bound = pl.pallas_call(
-        functools.partial(bound_kernel, sectors),
-        in_specs=[smem()] + [vmem()] * 3,
-        out_specs=vmem(),
-        out_shape=like,
+    y = lax.axis_index("y")
+    far = [lax.ppermute(lax.dynamic_slice_in_dim(wave_out, y * width, width), SEC + ("z1", "z0"), mirrored())]
+    for k in range(1, sectors):
+        far.append(lax.ppermute(far[0], ("core", "y"), [(i, i ^ k) for i in range(sectors)]))
+    place = jnp.stack([lax.axis_index("core"), y]).astype(jnp.int32).reshape(1, 2)
+    wave_out, bound = pl.pallas_call(
+        bound_kernel,
+        in_specs=[smem()] + [vmem()] * (2 + sectors),
+        out_specs=[hbm()] * 2,
+        out_shape=[like] * 2,
+        scratch_shapes=[pltpu.VMEM(wave.shape, jnp.float32), pltpu.SemaphoreType.DMA((sectors + 1,))],
         compiler_params=params(),
         cost_estimate=cost(12 * sectors * width**3, 16 * wave.size),
-    )(core.astype(jnp.int32).reshape(1, 1), wave_out, near, far)
+    )(place, wave_out, near, *far)
     return (wave_out.reshape(wave_in.shape), bound.reshape(wave_in.shape))
 
 

time: 144 us -> 140 us (0.972)
  waiting for transfers between devices: 44.6 us -> 35.8 us
  starting transfers between devices: 16.6 us -> 23.3 us
    ppermute x1 -> x4, starting transfers between devices: 1.28 us -> 11.1 us  [the longest x3 9.81 us: shards(): lax.ppermute(far[0], ('core', 'y'), [(i, i ^ k) for i in range(sectors)])]
    ppermute x1 -> x4, waiting for transfers between devices: 24.2 us -> 15.5 us  [the longest x1 10.4 us: shards(): lax.ppermute(lax.dynamic_slice_in_dim(wave_out, y * width, width), SEC +...]
    ppermute x1, starting transfers between devices: 3.26 us -> 0.09 us  [shards(): near = lax.ppermute(wave_out, 'core', SWAP)]
  transfers between devices with their start and end apart: 5 -> 8, of which waited for: 4 -> 6; matrix products, arithmetic and copies ran while one was open for 1% -> 1% of each run, Pallas kernels for 0% -> 0%
where the time goes in v3:
time: 140 us; the launch traced here: 139 us
  blocking collectives  60.4 us (43%)
  waiting for transfers between devices  35.8 us (26%)
  starting transfers between devices  23.3 us (17%)
  Pallas kernels  15.8 us (11%)
  local copies, waits for them, and re-layouts  1.56 us (1%)
    all_to_all x2, blocking collectives, gathered_sums(): lax.all_to_all(jnp.broadcast_to(piece[None], (ways,) + piece.shape), NEAR...  40.1 us
    all_to_all x1, blocking collectives, gathered_sums(): lax.all_to_all(partial.reshape(ways, rows // ways, width), NEAR, 0, 0)  20.4 us
    all_to_all x1, waiting for transfers between devices, gathered_sums(): lax.all_to_all(partial.reshape(ways, rows // ways, width), NEAR, 0, 0)  15.8 us
    ppermute x1, waiting for transfers between devices, shards(): lax.ppermute(lax.dynamic_slice_in_dim(wave_out, y * width, width), SEC +...  10.4 us
    ppermute x3, starting transfers between devices, shards(): lax.ppermute(far[0], ('core', 'y'), [(i, i ^ k) for i in range(sectors)])  9.81 us
    all_to_all x1, starting transfers between devices, gathered_sums(): lax.all_to_all(partial.reshape(ways, rows // ways, width), NEAR, 0, 0)  7.08 us
    pallas_call x1, Pallas kernels, first_sums(): pl.pallas_call(first_kernel, in_specs=[smem()] + [hbm()] * 3, out_specs=v...  6.77 us
    pallas_call x1, Pallas kernels, second_sums(): pl.pallas_call(second_kernel, in_specs=[smem()] + [vmem()] * 2 + [hbm()]...  5.67 us
  transfers between devices with their start and end apart: 8, of which 6 were waited for; matrix products, arithmetic and copies ran while one was open for 1% of the time, Pallas kernels for 0%

profile of v3, /device:TPU:0, one launch (start us, length us, event | category | flops | bytes accessed | tf_op | source)
XLA Modules:
  0.0 138.6 jit_solution(217542412128449874)
XLA Ops:
  0.6 0.0 copy-start.1
  0.6 0.6 copy-done.1
  1.3 0.0 copy-start.2
  1.3 6.8 %shard_map.59 = f32[1024,256]{1,0:T(8,128)} custom-call(s32[1,4]{1,0:T(1,128)S(1)} %copy-done.1, f32[1024,256]{1,0:T(8,128)} %bitcast.16, bf16[8,4,256,256]{3,2,1,0:T(8,128)(2,1)} %bitcast.19, bf16[8,4,256,256]{3,2,1,0:T(8,128)(2,1)} %bitcast.21), custom_call_target="tpu_custom_call" | custom-call | flops 2147483648 | bytes 8388608 | tf_op jit(solution)/shard_map/pallas_call | solution.py:192
  8.1 0.0 copy-start
  8.1 7.1 %all-to-all-start = ((f32[32,32,256]{2,1,0:T(8,128)}), f32[32,32,256]{2,1,0:T(8,128)S(1)}, u32[]{:S(2)}, u32[]{:S(2)}) async-start(f32[32,32,256]{2,1,0:T(8,128)} %bitcast.7), calls=%async_computation | async-start | bytes 2097152 | tf_op jit(solution)/shard_map/all_to_all | solution.py:228
  15.2 0.0 copy-done.2
  15.2 0.7 constant_dynamic-slice_fusion.1
  15.9 15.8 %all-to-all-done = f32[32,32,256]{2,1,0:T(8,128)S(1)} async-done(((f32[32,32,256]{2,1,0:T(8,128)}), f32[32,32,256]{2,1,0:T(8,128)S(1)}, u32[]{:S(2)}, u32[]{:S(2)}) %all-to-all-start) | async-done | bytes 1048608 | tf_op jit(solution)/shard_map/all_to_all | solution.py:228
  31.7 0.1 reduce_sum.18
  31.8 3.4 %collective-permute-start = (f32[32,256]{1,0:T(8,128)S(1)}, f32[32,256]{1,0:T(8,128)S(1)}, u32[]{:S(2)}, u32[]{:S(2)}) collective-permute-start(f32[32,256]{1,0:T(8,128)S(1)} %reduce_sum.18), channel_id=1, source_target_pairs={{0,32},{32,0},{1,33},{33,1},{2,34},{34,2},{3,35},{35,3},{4,36},{36... | collective-permute-start | bytes 98312 | tf_op jit(solution)/shard_map/ppermute | solution.py:229
  35.1 0.7 iota_compare_fusion
  35.8 1.2 collective-permute-done
  37.0 0.1 broadcast_in_dim.32
  37.1 20.8 %all_to_all.20 = f32[32,32,256]{2,1,0:T(8,128)S(1)} all-to-all(f32[32,32,256]{2,1,0:T(8,128)S(1)} %broadcast_in_dim.32), channel_id=1, replica_groups=mesh['zh'=2,'core'=2,'z1'=2,'z0'=2,'y'=4,'x'=4] {'z0','y','x'}, dimensions={0} | all-to-all | bytes 2097152 | tf_op jit(solution)/shard_map/all_to_all | solution.py:233
  58.0 0.0 copy-done
  58.0 5.7 %shard_map.60 = (f32[1024,256]{1,0:T(8,128)S(1)}, f32[1024,256]{1,0:T(8,128)S(1)}) custom-call(s32[1,4]{1,0:T(1,128)S(1)} %copy-done.2, f32[1024,256]{1,0:T(8,128)S(1)} %bitcast.17, f32[1024,256]{1,0:T(8,128)S(1)} %bitcast.15, bf16[8,4,256,256]{3,2,1,0:T(8,128)(2,1)} %bitcast.20, bf16[8,4,256,256]{3,2,1,0:T(8,128)(2,1)} %bitcast.22), custom_call_target="tpu_custom_call" | custom-call | flops 2147483648 | bytes 8388608 | tf_op jit(solution)/shard_map/pallas_call | solution.py:210
  63.6 20.4 %all_to_all.21 = f32[32,32,256]{2,1,0:T(8,128)S(1)} all-to-all(f32[32,32,256]{2,1,0:T(8,128)S(1)} %bitcast.18), channel_id=1, replica_groups=mesh['zh'=2,'core'=2,'z1'=2,'z0'=2,'y'=4,'x'=4] {'z0','y','x'}, dimensions={0} | all-to-all | bytes 2097152 | tf_op jit(solution)/shard_map/all_to_all | solution.py:228
  84.0 0.1 reduce_sum.19
  84.1 1.6 %collective-permute-start.1 = (f32[32,256]{1,0:T(8,128)S(1)}, f32[32,256]{1,0:T(8,128)S(1)}, u32[]{:S(2)}, u32[]{:S(2)}) collective-permute-start(f32[32,256]{1,0:T(8,128)S(1)} %reduce_sum.19), channel_id=1, source_target_pairs={{0,32},{32,0},{1,33},{33,1},{2,34},{34,2},{3,35},{35,3},{4,36},{36... | collective-permute-start | bytes 98312 | tf_op jit(solution)/shard_map/ppermute | solution.py:229
  85.7 3.3 %collective-permute-done.1 = f32[32,256]{1,0:T(8,128)S(1)} collective-permute-done((f32[32,256]{1,0:T(8,128)S(1)}, f32[32,256]{1,0:T(8,128)S(1)}, u32[]{:S(2)}, u32[]{:S(2)}) %collective-permute-start.1) | collective-permute-done | bytes 32800 | tf_op jit(solution)/shard_map/ppermute | solution.py:229
  89.0 0.1 broadcast_in_dim.33
  89.1 19.3 %all_to_all.22 = f32[32,32,256]{2,1,0:T(8,128)S(1)} all-to-all(f32[32,32,256]{2,1,0:T(8,128)S(1)} %broadcast_in_dim.33), channel_id=1, replica_groups=mesh['zh'=2,'core'=2,'z1'=2,'z0'=2,'y'=4,'x'=4] {'z0','y','x'}, dimensions={0} | all-to-all | bytes 2097152 | tf_op jit(solution)/shard_map/all_to_all | solution.py:233
  108.3 0.9 shard_map.61.wave_ref
  109.2 0.1 collective-permute-start.2
  109.3 1.3 collective-permute-start.3
  110.6 10.4 %collective-permute-done.3.refs_0_ = f32[256,256]{1,0:T(8,128)S(1)} collective-permute-done((f32[256,256]{1,0:T(8,128)S(1)}, f32[256,256]{1,0:T(8,128)S(1)}, u32[]{:S(2)}, u32[]{:S(2)}) %collective-permute-start.3) | collective-permute-done | bytes 262176 | tf_op jit(solution)/shard_map/ppermute | solution.py:254
  121.1 4.1 %collective-permute-start.6 = (f32[256,256]{1,0:T(8,128)S(1)}, f32[256,256]{1,0:T(8,128)S(1)}, u32[]{:S(2)}, u32[]{:S(2)}) collective-permute-start(f32[256,256]{1,0:T(8,128)S(1)} %collective-permute-done.3.refs_0_), channel_id=1, source_target_pairs={{0,12},{4,8},{8,4},{12,0},{1,13},{5,9},{9,5},{13,1},{2,14},{6,10},... | collective-permute-start | bytes 786440 | tf_op jit(solution)/shard_map/ppermute | solution.py:256
  125.1 2.3 %collective-permute-start.5 = (f32[256,256]{1,0:T(8,128)S(1)}, f32[256,256]{1,0:T(8,128)S(1)}, u32[]{:S(2)}, u32[]{:S(2)}) collective-permute-start(f32[256,256]{1,0:T(8,128)S(1)} %collective-permute-done.3.refs_0_), channel_id=1, source_target_pairs={{0,8},{4,12},{8,0},{12,4},{1,9},{5,13},{9,1},{13,5},{2,10},{6,14},... | collective-permute-start | bytes 786440 | tf_op jit(solution)/shard_map/ppermute | solution.py:256
  127.5 3.4 %collective-permute-start.4 = (f32[256,256]{1,0:T(8,128)S(1)}, f32[256,256]{1,0:T(8,128)S(1)}, u32[]{:S(2)}, u32[]{:S(2)}) collective-permute-start(f32[256,256]{1,0:T(8,128)S(1)} %collective-permute-done.3.refs_0_), channel_id=1, source_target_pairs={{0,4},{4,0},{8,12},{12,8},{1,5},{5,1},{9,13},{13,9},{2,6},{6,2},{1... | collective-permute-start | bytes 786440 | tf_op jit(solution)/shard_map/ppermute | solution.py:256
  130.9 0.1 add_bitcast_fusion.place_ref
  131.0 0.0 collective-permute-done.6.refs_3_
  131.0 3.9 %collective-permute-done.5.refs_2_ = f32[256,256]{1,0:T(8,128)S(1)} collective-permute-done((f32[256,256]{1,0:T(8,128)S(1)}, f32[256,256]{1,0:T(8,128)S(1)}, u32[]{:S(2)}, u32[]{:S(2)}) %collective-permute-start.5) | collective-permute-done | bytes 262176 | tf_op jit(solution)/shard_map/ppermute | solution.py:256
  134.9 1.2 collective-permute-done.4.refs_1_
  136.1 0.0 collective-permute-done.2.near_ref
  136.1 2.5 %shard_map.62 = (f32[1024,256]{1,0:T(8,128)}, f32[1024,256]{1,0:T(8,128)}) custom-call(s32[1,2]{1,0:T(1,128)S(1)} %add_bitcast_fusion.place_ref, f32[1024,256]{1,0:T(8,128)S(1)} %shard_map.61.wave_ref, f32[1024,256]{1,0:T(8,128)S(1)} %collective-permute-done.2.near_ref, f32[256,256]{1,0:T(8,128)S(1)} %collective-permute-done.3.refs_0_, ...), custom_call_target="tpu_custom_call" | custom-call | flops 805306368 | bytes 4194304 | tf_op jit(solution)/shard_map/pallas_call | solution.py:258
  (3 shorter events, 0.0 us)
Async XLA Ops:
  0.6 0.7 copy-start.1
  1.3 13.9 %copy-start.2 = (s32[1,4]{1,0:T(1,128)S(1)}, s32[1,4]{1,0:T(1,128)}, u32[]{:S(2)}) copy-start(s32[1,4]{1,0:T(1,128)} %kept_ref.3) | copy-start | bytes 52
  8.1 49.9 %copy-start = (f32[1,4,256,256]{3,2,1,0:T(8,128)S(1)}, f32[1,4,256,256]{3,2,1,0:T(8,128)}, u32[]{:S(2)}) copy-start(f32[1,4,256,256]{3,2,1,0:T(8,128)} %param.4) | copy-start | bytes 3145732
  8.1 23.6 %all-to-all-start = ((f32[32,32,256]{2,1,0:T(8,128)}), f32[32,32,256]{2,1,0:T(8,128)S(1)}, u32[]{:S(2)}, u32[]{:S(2)}) async-start(f32[32,32,256]{2,1,0:T(8,128)} %bitcast.7), calls=%async_computation | async-start | bytes 2097152 | tf_op jit(solution)/shard_map/all_to_all | solution.py:228
  31.8 5.3 %collective-permute-start = (f32[32,256]{1,0:T(8,128)S(1)}, f32[32,256]{1,0:T(8,128)S(1)}, u32[]{:S(2)}, u32[]{:S(2)}) collective-permute-start(f32[32,256]{1,0:T(8,128)S(1)} %reduce_sum.18), channel_id=1, source_target_pairs={{0,32},{32,0},{1,33},{33,1},{2,34},{34,2},{3,35},{35,3},{4,36},{36... | collective-permute-start | bytes 98312 | tf_op jit(solution)/shard_map/ppermute | solution.py:229
  84.1 4.9 %collective-permute-start.1 = (f32[32,256]{1,0:T(8,128)S(1)}, f32[32,256]{1,0:T(8,128)S(1)}, u32[]{:S(2)}, u32[]{:S(2)}) collective-permute-start(f32[32,256]{1,0:T(8,128)S(1)} %reduce_sum.19), channel_id=1, source_target_pairs={{0,32},{32,0},{1,33},{33,1},{2,34},{34,2},{3,35},{35,3},{4,36},{36... | collective-permute-start | bytes 98312 | tf_op jit(solution)/shard_map/ppermute | solution.py:229
  109.2 26.9 %collective-permute-start.2 = (f32[1024,256]{1,0:T(8,128)S(1)}, f32[1024,256]{1,0:T(8,128)S(1)}, u32[]{:S(2)}, u32[]{:S(2)}) collective-permute-start(f32[1024,256]{1,0:T(8,128)S(1)} %shard_map.61.wave_ref), channel_id=1, source_target_pairs={{0,64},{64,0},{1,65},{65,1},{2,66},{66,2},{3,67},{67,3},{4,68},{68... | collective-permute-start | bytes 3145736 | tf_op jit(solution)/shard_map/ppermute | solution.py:252
  109.3 11.7 %collective-permute-start.3 = (f32[256,256]{1,0:T(8,128)S(1)}, f32[256,256]{1,0:T(8,128)S(1)}, u32[]{:S(2)}, u32[]{:S(2)}) collective-permute-start(f32[256,256]{1,0:T(8,128)S(1)} %constant_dynamic-slice_fusion), channel_id=1, source_target_pairs={{64,176},{80,160},{96,144},{112,128},{192,48},{208,32},{224,16},{2... | collective-permute-start | bytes 786440 | tf_op jit(solution)/shard_map/ppermute | solution.py:254
  121.1 9.9 %collective-permute-start.6 = (f32[256,256]{1,0:T(8,128)S(1)}, f32[256,256]{1,0:T(8,128)S(1)}, u32[]{:S(2)}, u32[]{:S(2)}) collective-permute-start(f32[256,256]{1,0:T(8,128)S(1)} %collective-permute-done.3.refs_0_), channel_id=1, source_target_pairs={{0,12},{4,8},{8,4},{12,0},{1,13},{5,9},{9,5},{13,1},{2,14},{6,10},... | collective-permute-start | bytes 786440 | tf_op jit(solution)/shard_map/ppermute | solution.py:256
  125.1 9.8 %collective-permute-start.5 = (f32[256,256]{1,0:T(8,128)S(1)}, f32[256,256]{1,0:T(8,128)S(1)}, u32[]{:S(2)}, u32[]{:S(2)}) collective-permute-start(f32[256,256]{1,0:T(8,128)S(1)} %collective-permute-done.3.refs_0_), channel_id=1, source_target_pairs={{0,8},{4,12},{8,0},{12,4},{1,9},{5,13},{9,1},{13,5},{2,10},{6,14},... | collective-permute-start | bytes 786440 | tf_op jit(solution)/shard_map/ppermute | solution.py:256
  127.5 8.6 %collective-permute-start.4 = (f32[256,256]{1,0:T(8,128)S(1)}, f32[256,256]{1,0:T(8,128)S(1)}, u32[]{:S(2)}, u32[]{:S(2)}) collective-permute-start(f32[256,256]{1,0:T(8,128)S(1)} %collective-permute-done.3.refs_0_), channel_id=1, source_target_pairs={{0,4},{4,0},{8,12},{12,8},{1,5},{5,1},{9,13},{13,9},{2,6},{6,2},{1... | collective-permute-start | bytes 786440 | tf_op jit(solution)/shard_map/ppermute | solution.py:256

commit v4 on v3

--- a/solution.py
+++ b/solution.py
@@ -25,9 +25,8 @@
     return pairs
 
 
-def masked(block, kept):
-    cols = lax.broadcasted_iota(jnp.int32, block.shape, block.ndim - 1)
-    return jnp.where(cols < kept, block, 0.0)
+def spread(mask, rows):
+    return jnp.concatenate([mask] * (rows // mask.shape[0]), axis=0)
 
 
 def folded(block):
@@ -83,14 +82,18 @@
     return started
 
 
-def first_kernel(kept_ref, wave_hbm, left_hbm, right_hbm, out_ref, left_ref, right_ref, wave_ref, sems):
-    sectors, width = kept_ref.shape[1], wave_ref.shape[1]
+def first_kernel(
+    kept_hbm, wave_hbm, left_hbm, right_hbm, out_ref, state_ref, mask_ref, left_ref, right_ref, kept_ref, sems, kept_sem
+):
+    sectors, width = kept_ref.shape[1], state_ref.shape[1]
+    kept_copy = pltpu.make_async_copy(kept_hbm, kept_ref, kept_sem)
+    kept_copy.start()
     parts = [pl.ds(s * width, width) for s in range(sectors)]
     copies = fetch(
         [
             (
                 [
-                    (wave_hbm.at[parts[s]], wave_ref.at[parts[s]]),
+                    (wave_hbm.at[parts[s]], state_ref.at[parts[s]]),
                     (right_hbm.at[:, s], right_ref.at[:, s]),
                     (left_hbm.at[:, s], left_ref.at[:, s]),
                 ],
@@ -99,16 +102,21 @@
             for s in range(sectors)
         ]
     )
+    kept_copy.wait()
+    for s in range(sectors):
+        cols = lax.broadcasted_iota(jnp.int32, mask_ref.shape[1:], 1)
+        mask_ref[s] = jnp.where(cols < kept_ref[0, s], 1.0, 0.0)
     for s in range(sectors):
         for copy in copies[s]:
             copy.wait()
-        out_ref[parts[s], :] = sector_sums(masked(wave_ref[parts[s], :], kept_ref[0, s]), left_ref, right_ref, s)
-
-
-def second_kernel(kept_ref, wave_ref, sigma_ref, left_hbm, right_hbm, out_ref, state_ref, left_ref, right_ref, sems):
-    sectors = kept_ref.shape[1]
-    rows, width = wave_ref.shape
-    share = rows // CHUNK // sectors
+        state = spread(mask_ref[s], width) * state_ref[parts[s], :]
+        state_ref[parts[s], :] = state
+        out_ref[parts[s], :] = sector_sums(state, left_ref, right_ref, s)
+
+
+def second_kernel(old_ref, sigma_ref, left_hbm, right_hbm, out_ref, state_ref, left_ref, right_ref, sems):
+    rows, width = old_ref.shape
+    sectors = rows // width
     copies = fetch(
         [
             (
@@ -118,13 +126,7 @@
             for s in range(sectors)
         ]
     )
-    update(
-        rows,
-        width,
-        lambda i: masked(wave_ref[chunk(i), :], kept_ref[0, i // share]),
-        lambda i: sigma_ref[chunk(i), :],
-        state_ref,
-    )
+    update(rows, width, lambda i: old_ref[chunk(i), :], lambda i: sigma_ref[chunk(i), :], state_ref)
     for s in range(sectors):
         part = pl.ds(s * width, width)
         for copy in copies[s]:
@@ -137,30 +139,53 @@
     update(rows, width, lambda i: state_ref[chunk(i), :], lambda i: sigma_ref[chunk(i), :], out_ref)
 
 
-def bound_kernel(place_ref, wave_ref, near_ref, *refs):
-    sectors = len(refs) - 4
-    far_refs, (wave_out, bound_out, bound_ref, sems) = refs[:sectors], refs[sectors:]
-    width = wave_ref.shape[1]
-    leaving = pltpu.make_async_copy(wave_ref, wave_out, sems.at[sectors])
+def copies_kernel(here_ref, there_ref, mask_ref, out_ref):
+    ways = out_ref.shape[0]
+    sector = lax.axis_index(NEAR) * mask_ref.shape[0] // ways
+    piece = spread(mask_ref[sector], here_ref.shape[0]) * (here_ref[...] + there_ref[...])
+    for i in range(ways):
+        out_ref[i] = piece
+
+
+def halves(block):
+    high = block.astype(jnp.bfloat16)
+    return high, (block - high.astype(jnp.float32)).astype(jnp.bfloat16)
+
+
+def near_kernel(wave_ref, near_ref, wave_out, product_ref, high_ref, low_ref, sem):
+    leaving = pltpu.make_async_copy(wave_ref, wave_out, sem)
     leaving.start()
+    rows, width = wave_ref.shape
+    for s in range(rows // width):
+        part = pl.ds(s * width, width)
+        wave = wave_ref[part, :].T
+        high_ref[part, :], low_ref[part, :] = halves(wave)
+        product_ref[part, :] = jnp.dot(
+            wave, near_ref[part, :], precision=lax.Precision.HIGHEST, preferred_element_type=jnp.float32
+        )
+    leaving.wait()
+
+
+def bound_kernel(place_ref, product_ref, high_ref, low_ref, *refs):
+    sectors = len(refs) - 3
+    far_refs, (out_hbm, bound_ref, sems) = refs[:sectors], refs[sectors:]
+    width = product_ref.shape[1]
     even = place_ref[0, 0] == 0
     copies = []
     for k in range(sectors):
         rows = pl.ds(pl.multiple_of((place_ref[0, 1] ^ k) * width, width), width)
-        near = near_ref[rows, :]
-        partner = near + jnp.where(even, far_refs[k][...], near)
-        bound_ref[rows, :] = lax.dot_general(
-            wave_ref[rows, :],
-            partner,
-            (((0,), (0,)), ((), ())),
-            precision=lax.Precision.HIGHEST,
-            preferred_element_type=jnp.float32,
-        ) / math.sqrt(width)
-        copies.append(pltpu.make_async_copy(bound_ref.at[rows], bound_out.at[rows], sems.at[k]))
-        copies[k].start()
+        far_high, far_low = halves(far_refs[k][...])
+        near = product_ref[rows, :]
+        far = jnp.dot(high_ref[rows, :], far_high, preferred_element_type=jnp.float32)
+        far += jnp.dot(high_ref[rows, :], far_low, preferred_element_type=jnp.float32)
+        far += jnp.dot(low_ref[rows, :], far_high, preferred_element_type=jnp.float32)
+        bound_ref[rows, :] = (near + jnp.where(even, far, near)) / math.sqrt(width)
+        copies.append(pltpu.make_async_copy(bound_ref.at[rows], out_hbm.at[rows], sems.at[k]))
+        if k % 2:
+            copies[k - 1].start()
+            copies[k].start()
     for copy in copies:
         copy.wait()
-    leaving.wait()
 
 
 def params():
@@ -191,27 +216,29 @@
     terms, sectors, width, _ = left.shape
     return pl.pallas_call(
         first_kernel,
-        in_specs=[smem()] + [hbm()] * 3,
-        out_specs=vmem(),
-        out_shape=jax.ShapeDtypeStruct(wave.shape, jnp.float32),
+        in_specs=[hbm()] * 4,
+        out_specs=[vmem()] * 3,
+        out_shape=[jax.ShapeDtypeStruct(wave.shape, jnp.float32)] * 2
+        + [jax.ShapeDtypeStruct((sectors, 8, width), jnp.float32)],
         scratch_shapes=[
             pltpu.VMEM(left.shape, left.dtype),
             pltpu.VMEM(right.shape, right.dtype),
-            pltpu.VMEM(wave.shape, wave.dtype),
+            pltpu.SMEM(kept.shape, kept.dtype),
             pltpu.SemaphoreType.DMA((sectors, 3)),
+            pltpu.SemaphoreType.DMA,
         ],
         compiler_params=params(),
         cost_estimate=cost(4 * terms * sectors * width**3, 4 * left.size),
-    )(kept, *in_hbm(wave, left, right))
-
-
-def second_sums(kept, wave, sigma, left, right):
+    )(*in_hbm(kept, wave, left, right))
+
+
+def second_sums(state, sigma, left, right):
     terms, sectors, width, _ = left.shape
     return pl.pallas_call(
         second_kernel,
-        in_specs=[smem()] + [vmem()] * 2 + [hbm()] * 2,
+        in_specs=[vmem()] * 2 + [hbm()] * 2,
         out_specs=[vmem()] * 2,
-        out_shape=[jax.ShapeDtypeStruct(wave.shape, jnp.float32)] * 2,
+        out_shape=[jax.ShapeDtypeStruct(state.shape, jnp.float32)] * 2,
         scratch_shapes=[
             pltpu.VMEM(left.shape, left.dtype),
             pltpu.VMEM(right.shape, right.dtype),
@@ -219,18 +246,22 @@
         ],
         compiler_params=params(),
         cost_estimate=cost(4 * terms * sectors * width**3, 4 * left.size),
-    )(kept, wave, sigma, *in_hbm(left, right))
-
-
-def gathered_sums(partial, kept):
+    )(state, sigma, *in_hbm(left, right))
+
+
+def gathered_sums(partial, mask):
     rows, width = partial.shape
     ways = lax.axis_size(NEAR)
     piece = lax.all_to_all(partial.reshape(ways, rows // ways, width), NEAR, 0, 0).sum(0)
-    piece = piece + lax.ppermute(piece, "z1", SWAP)
-    sector = lax.axis_index(NEAR) * kept.shape[1] // ways
-    cols = jnp.arange(width, dtype=jnp.int32)
-    piece = jnp.where(cols[None, :] < kept[0, sector], piece, 0.0)
-    return lax.all_to_all(jnp.broadcast_to(piece[None], (ways,) + piece.shape), NEAR, 0, 0).reshape(rows, width)
+    copies = pl.pallas_call(
+        copies_kernel,
+        in_specs=[vmem()] * 3,
+        out_specs=vmem(),
+        out_shape=jax.ShapeDtypeStruct((ways, rows // ways, width), jnp.float32),
+        compiler_params=params(),
+        cost_estimate=cost(2 * piece.size, 4 * partial.size),
+    )(piece, lax.ppermute(piece, "z1", SWAP), mask)
+    return lax.all_to_all(copies, NEAR, 0, 0).reshape(rows, width)
 
 
 def shards(wave_in, kept, left_ops, right_ops):
@@ -239,8 +270,8 @@
     like = jax.ShapeDtypeStruct(wave.shape, jnp.float32)
 
     left, right = left_ops[0], right_ops[0]
-    sums = first_sums(kept, wave, left, right)
-    sums, state = second_sums(kept, wave, gathered_sums(sums, kept), left, right)
+    sums, state, mask = first_sums(kept, wave, left, right)
+    sums, state = second_sums(state, gathered_sums(sums, mask), left, right)
     wave_out = pl.pallas_call(
         own_kernel,
         in_specs=[vmem()] * 2,
@@ -248,22 +279,31 @@
         out_shape=like,
         compiler_params=params(),
         cost_estimate=cost(12 * wave.size, 12 * wave.size),
-    )(state, gathered_sums(sums, kept))
+    )(state, gathered_sums(sums, mask))
     near = lax.ppermute(wave_out, "core", SWAP)
     y = lax.axis_index("y")
     far = [lax.ppermute(lax.dynamic_slice_in_dim(wave_out, y * width, width), SEC + ("z1", "z0"), mirrored())]
     for k in range(1, sectors):
         far.append(lax.ppermute(far[0], ("core", "y"), [(i, i ^ k) for i in range(sectors)]))
     place = jnp.stack([lax.axis_index("core"), y]).astype(jnp.int32).reshape(1, 2)
-    wave_out, bound = pl.pallas_call(
+    wave_out, *products = pl.pallas_call(
+        near_kernel,
+        in_specs=[vmem()] * 2,
+        out_specs=[hbm()] + [vmem()] * 3,
+        out_shape=[like, like] + [jax.ShapeDtypeStruct(wave.shape, jnp.bfloat16)] * 2,
+        scratch_shapes=[pltpu.SemaphoreType.DMA],
+        compiler_params=params(),
+        cost_estimate=cost(12 * sectors * width**3, 16 * wave.size),
+    )(wave_out, near)
+    bound = pl.pallas_call(
         bound_kernel,
-        in_specs=[smem()] + [vmem()] * (2 + sectors),
-        out_specs=[hbm()] * 2,
-        out_shape=[like] * 2,
-        scratch_shapes=[pltpu.VMEM(wave.shape, jnp.float32), pltpu.SemaphoreType.DMA((sectors + 1,))],
-        compiler_params=params(),
-        cost_estimate=cost(12 * sectors * width**3, 16 * wave.size),
-    )(place, wave_out, near, *far)
+        in_specs=[smem()] + [vmem()] * (3 + sectors),
+        out_specs=hbm(),
+        out_shape=like,
+        scratch_shapes=[pltpu.VMEM(wave.shape, jnp.float32), pltpu.SemaphoreType.DMA((sectors,))],
+        compiler_params=params(),
+        cost_estimate=cost(6 * sectors * width**3, 16 * wave.size),
+    )(place, *products, *far)
     return (wave_out.reshape(wave_in.shape), bound.reshape(wave_in.shape))
 
 

time: 140 us -> 137 us (0.979)
  blocking collectives: 60.4 us -> 83.7 us
  waiting for transfers between devices: 35.8 us -> 20.7 us
  starting transfers between devices: 23.3 us -> 16.8 us
  local copies, waits for them, and re-layouts: 1.56 us -> 0.02 us
    all_to_all x1 -> x2, blocking collectives: 20.4 us -> 43.6 us  [gathered_sums(): lax.all_to_all(partial.reshape(ways, rows // ways, width), NEAR, 0, 0)]
    all_to_all x1 -> x0, waiting for transfers between devices: 15.8 us -> none  [gathered_sums(): lax.all_to_all(partial.reshape(ways, rows // ways, width), NEAR, 0, 0)]
    all_to_all x1 -> x0, starting transfers between devices: 7.08 us -> none  [gathered_sums(): lax.all_to_all(partial.reshape(ways, rows // ways, width), NEAR, 0, 0)]
    pallas_call x3 -> x6, Pallas kernels: 15 us -> 13.9 us  [the longest x1 5.27 us: first_sums(): pl.pallas_call(first_kernel, in_specs=[hbm()] * 4, out_specs=[vmem()] * 3...]
  transfers between devices with their start and end apart: 8 -> 7, of which waited for: 6 -> 5; matrix products, arithmetic and copies ran while one was open for 1% -> 0% of each run, Pallas kernels for 0% -> 1%
where the time goes in v4:
time: 137 us
  blocking collectives  83.7 us (61%)
  waiting for transfers between devices  20.7 us (15%)
  starting transfers between devices  16.8 us (12%)
  Pallas kernels  14.7 us (11%)
    all_to_all x2, blocking collectives, gathered_sums(): lax.all_to_all(partial.reshape(ways, rows // ways, width), NEAR, 0, 0)  43.6 us
    all_to_all x2, blocking collectives, gathered_sums(): return lax.all_to_all(copies, NEAR, 0, 0).reshape(rows, width)  40.1 us
    ppermute x3, starting transfers between devices, shards(): lax.ppermute(far[0], ('core', 'y'), [(i, i ^ k) for i in range(sectors)])  10.4 us
    ppermute x1, waiting for transfers between devices, shards(): lax.ppermute(lax.dynamic_slice_in_dim(wave_out, y * width, width), SEC +...  10.4 us
    pallas_call x1, Pallas kernels, first_sums(): pl.pallas_call(first_kernel, in_specs=[hbm()] * 4, out_specs=[vmem()] * 3...  5.27 us
    ppermute x2, waiting for transfers between devices, gathered_sums(): lax.ppermute(piece, 'z1', SWAP)  5.15 us
    ppermute x3, waiting for transfers between devices, shards(): lax.ppermute(far[0], ('core', 'y'), [(i, i ^ k) for i in range(sectors)])  5.14 us
    pallas_call x1, Pallas kernels, second_sums(): pl.pallas_call(second_kernel, in_specs=[vmem()] * 2 + [hbm()] * 2, out_sp...  5.13 us
  transfers between devices with their start and end apart: 7, of which 5 were waited for; matrix products, arithmetic and copies ran while one was open for 0% of the time, Pallas kernels for 1%

profile of v4, /device:TPU:0, one launch (start us, length us, event | category | flops | bytes accessed | tf_op | source)
XLA Modules:
  0.0 136.9 jit_solution(14824849484721339766)
XLA Ops:
  0.6 5.3 %shard_map.59 = (f32[1024,256]{1,0:T(8,128)S(1)}, f32[1024,256]{1,0:T(8,128)S(1)}, f32[4,8,256]{2,1,0:T(8,128)S(1)}) custom-call(s32[1,4]{1,0:T(1,128)} %kept_hbm.1, f32[1024,256]{1,0:T(8,128)} %bitcast.21, bf16[8,4,256,256]{3,2,1,0:T(8,128)(2,1)} %bitcast.17, bf16[8,4,256,256]{3,2,1,0:T(8,128)(2,1)} %bitcast.19), custom_call_target="tpu_custom_call" | custom-call | flops 2147483648 | bytes 8388608 | tf_op jit(solution)/shard_map/pallas_call | solution.py:217
  5.9 23.3 %all_to_all.20 = f32[32,32,256]{2,1,0:T(8,128)S(1)} all-to-all(f32[32,32,256]{2,1,0:T(8,128)S(1)} %bitcast.16), channel_id=1, replica_groups=mesh['zh'=2,'core'=2,'z1'=2,'z0'=2,'y'=4,'x'=4] {'z0','y','x'}, dimensions={0} | all-to-all | bytes 2097152 | tf_op jit(solution)/shard_map/all_to_all | solution.py:255
  29.2 0.1 reduce_sum.18.here_ref
  29.2 3.4 %collective-permute-start = (f32[32,256]{1,0:T(8,128)S(1)}, f32[32,256]{1,0:T(8,128)S(1)}, u32[]{:S(2)}, u32[]{:S(2)}) collective-permute-start(f32[32,256]{1,0:T(8,128)S(1)} %reduce_sum.18.here_ref), channel_id=1, source_target_pairs={{0,32},{32,0},{1,33},{33,1},{2,34},{34,2},{3,35},{35,3},{4,36},{36... | collective-permute-start | bytes 98312 | tf_op jit(solution)/shard_map/ppermute | solution.py:263
  32.6 1.9 %collective-permute-done.there_ref = f32[32,256]{1,0:T(8,128)S(1)} collective-permute-done((f32[32,256]{1,0:T(8,128)S(1)}, f32[32,256]{1,0:T(8,128)S(1)}, u32[]{:S(2)}, u32[]{:S(2)}) %collective-permute-start) | collective-permute-done | bytes 32800 | tf_op jit(solution)/shard_map/ppermute | solution.py:263
  34.5 0.1 shard_map.60
  34.6 20.8 %all_to_all.21 = f32[32,32,256]{2,1,0:T(8,128)S(1)} all-to-all(f32[32,32,256]{2,1,0:T(8,128)S(1)} %shard_map.60), channel_id=1, replica_groups=mesh['zh'=2,'core'=2,'z1'=2,'z0'=2,'y'=4,'x'=4] {'z0','y','x'}, dimensions={0} | all-to-all | bytes 2097152 | tf_op jit(solution)/shard_map/all_to_all | solution.py:264
  55.4 5.1 %shard_map.61 = (f32[1024,256]{1,0:T(8,128)S(1)}, f32[1024,256]{1,0:T(8,128)S(1)}) custom-call(f32[1024,256]{1,0:T(8,128)S(1)} %get-tuple-element.11.old_ref, f32[1024,256]{1,0:T(8,128)S(1)} %bitcast.13, bf16[8,4,256,256]{3,2,1,0:T(8,128)(2,1)} %bitcast.18, bf16[8,4,256,256]{3,2,1,0:T(8,128)(2,1)} %bitcast.20), custom_call_target="tpu_custom_call" | custom-call | flops 2147483648 | bytes 8388608 | tf_op jit(solution)/shard_map/pallas_call | solution.py:237
  60.6 20.4 %all_to_all.22 = f32[32,32,256]{2,1,0:T(8,128)S(1)} all-to-all(f32[32,32,256]{2,1,0:T(8,128)S(1)} %bitcast.15), channel_id=1, replica_groups=mesh['zh'=2,'core'=2,'z1'=2,'z0'=2,'y'=4,'x'=4] {'z0','y','x'}, dimensions={0} | all-to-all | bytes 2097152 | tf_op jit(solution)/shard_map/all_to_all | solution.py:255
  80.9 0.1 reduce_sum.19.here_ref
  81.0 1.6 %collective-permute-start.1 = (f32[32,256]{1,0:T(8,128)S(1)}, f32[32,256]{1,0:T(8,128)S(1)}, u32[]{:S(2)}, u32[]{:S(2)}) collective-permute-start(f32[32,256]{1,0:T(8,128)S(1)} %reduce_sum.19.here_ref), channel_id=1, source_target_pairs={{0,32},{32,0},{1,33},{33,1},{2,34},{34,2},{3,35},{35,3},{4,36},{36... | collective-permute-start | bytes 98312 | tf_op jit(solution)/shard_map/ppermute | solution.py:263
  82.6 3.3 %collective-permute-done.1.there_ref = f32[32,256]{1,0:T(8,128)S(1)} collective-permute-done((f32[32,256]{1,0:T(8,128)S(1)}, f32[32,256]{1,0:T(8,128)S(1)}, u32[]{:S(2)}, u32[]{:S(2)}) %collective-permute-start.1) | collective-permute-done | bytes 32800 | tf_op jit(solution)/shard_map/ppermute | solution.py:263
  85.9 0.1 shard_map.62
  86.0 19.3 %all_to_all.23 = f32[32,32,256]{2,1,0:T(8,128)S(1)} all-to-all(f32[32,32,256]{2,1,0:T(8,128)S(1)} %shard_map.62), channel_id=1, replica_groups=mesh['zh'=2,'core'=2,'z1'=2,'z0'=2,'y'=4,'x'=4] {'z0','y','x'}, dimensions={0} | all-to-all | bytes 2097152 | tf_op jit(solution)/shard_map/all_to_all | solution.py:264
  105.3 0.9 shard_map.63.wave_ref
  106.1 0.1 collective-permute-start.2
  106.3 1.3 collective-permute-start.3
  107.6 10.4 %collective-permute-done.3.refs_0_ = f32[256,256]{1,0:T(8,128)S(1)} collective-permute-done((f32[256,256]{1,0:T(8,128)S(1)}, f32[256,256]{1,0:T(8,128)S(1)}, u32[]{:S(2)}, u32[]{:S(2)}) %collective-permute-start.3) | collective-permute-done | bytes 262176 | tf_op jit(solution)/shard_map/ppermute | solution.py:285
  118.0 2.4 %collective-permute-start.4 = (f32[256,256]{1,0:T(8,128)S(1)}, f32[256,256]{1,0:T(8,128)S(1)}, u32[]{:S(2)}, u32[]{:S(2)}) collective-permute-start(f32[256,256]{1,0:T(8,128)S(1)} %collective-permute-done.3.refs_0_), channel_id=1, source_target_pairs={{0,4},{4,0},{8,12},{12,8},{1,5},{5,1},{9,13},{13,9},{2,6},{6,2},{1... | collective-permute-start | bytes 786440 | tf_op jit(solution)/shard_map/ppermute | solution.py:287
  120.4 5.0 %collective-permute-start.5 = (f32[256,256]{1,0:T(8,128)S(1)}, f32[256,256]{1,0:T(8,128)S(1)}, u32[]{:S(2)}, u32[]{:S(2)}) collective-permute-start(f32[256,256]{1,0:T(8,128)S(1)} %collective-permute-done.3.refs_0_), channel_id=1, source_target_pairs={{0,8},{4,12},{8,0},{12,4},{1,9},{5,13},{9,1},{13,5},{2,10},{6,14},... | collective-permute-start | bytes 786440 | tf_op jit(solution)/shard_map/ppermute | solution.py:287
  125.4 3.0 %collective-permute-start.6 = (f32[256,256]{1,0:T(8,128)S(1)}, f32[256,256]{1,0:T(8,128)S(1)}, u32[]{:S(2)}, u32[]{:S(2)}) collective-permute-start(f32[256,256]{1,0:T(8,128)S(1)} %collective-permute-done.3.refs_0_), channel_id=1, source_target_pairs={{0,12},{4,8},{8,4},{12,0},{1,13},{5,9},{9,5},{13,1},{2,14},{6,10},... | collective-permute-start | bytes 786440 | tf_op jit(solution)/shard_map/ppermute | solution.py:287
  128.4 0.1 add_bitcast_fusion.place_ref
  128.5 0.0 collective-permute-done.2.near_ref
  128.5 1.3 shard_map.64
  129.8 0.0 collective-permute-done.4.refs_1_
  129.8 0.9 collective-permute-done.5.refs_2_
  130.7 4.3 %collective-permute-done.6.refs_3_ = f32[256,256]{1,0:T(8,128)S(1)} collective-permute-done((f32[256,256]{1,0:T(8,128)S(1)}, f32[256,256]{1,0:T(8,128)S(1)}, u32[]{:S(2)}, u32[]{:S(2)}) %collective-permute-start.6) | collective-permute-done | bytes 262176 | tf_op jit(solution)/shard_map/ppermute | solution.py:287
  134.9 2.0 %shard_map.65 = f32[1024,256]{1,0:T(8,128)} custom-call(s32[1,2]{1,0:T(1,128)S(1)} %add_bitcast_fusion.place_ref, f32[1024,256]{1,0:T(8,128)S(1)} %get-tuple-element.17.product_ref, bf16[1024,256]{1,0:T(8,128)(2,1)S(1)} %get-tuple-element.18.high_ref, bf16[1024,256]{1,0:T(8,128)(2,1)S(1)} %get-tuple-element.19.low_ref, ...), custom_call_target="tpu_custom_call" | custom-call | flops 402653184 | bytes 4194304 | tf_op jit(solution)/shard_map/pallas_call | solution.py:298
  (1 shorter events, 0.0 us)
Async XLA Ops:
  29.2 5.3 %collective-permute-start = (f32[32,256]{1,0:T(8,128)S(1)}, f32[32,256]{1,0:T(8,128)S(1)}, u32[]{:S(2)}, u32[]{:S(2)}) collective-permute-start(f32[32,256]{1,0:T(8,128)S(1)} %reduce_sum.18.here_ref), channel_id=1, source_target_pairs={{0,32},{32,0},{1,33},{33,1},{2,34},{34,2},{3,35},{35,3},{4,36},{36... | collective-permute-start | bytes 98312 | tf_op jit(solution)/shard_map/ppermute | solution.py:263
  81.0 4.9 %collective-permute-start.1 = (f32[32,256]{1,0:T(8,128)S(1)}, f32[32,256]{1,0:T(8,128)S(1)}, u32[]{:S(2)}, u32[]{:S(2)}) collective-permute-start(f32[32,256]{1,0:T(8,128)S(1)} %reduce_sum.19.here_ref), channel_id=1, source_target_pairs={{0,32},{32,0},{1,33},{33,1},{2,34},{34,2},{3,35},{35,3},{4,36},{36... | collective-permute-start | bytes 98312 | tf_op jit(solution)/shard_map/ppermute | solution.py:263
  106.1 22.4 %collective-permute-start.2 = (f32[1024,256]{1,0:T(8,128)S(1)}, f32[1024,256]{1,0:T(8,128)S(1)}, u32[]{:S(2)}, u32[]{:S(2)}) collective-permute-start(f32[1024,256]{1,0:T(8,128)S(1)} %shard_map.63.wave_ref), channel_id=1, source_target_pairs={{0,64},{64,0},{1,65},{65,1},{2,66},{66,2},{3,67},{67,3},{4,68},{68... | collective-permute-start | bytes 3145736 | tf_op jit(solution)/shard_map/ppermute | solution.py:283
  106.3 11.7 %collective-permute-start.3 = (f32[256,256]{1,0:T(8,128)S(1)}, f32[256,256]{1,0:T(8,128)S(1)}, u32[]{:S(2)}, u32[]{:S(2)}) collective-permute-start(f32[256,256]{1,0:T(8,128)S(1)} %constant_dynamic-slice_fusion), channel_id=1, source_target_pairs={{64,176},{80,160},{96,144},{112,128},{192,48},{208,32},{224,16},{2... | collective-permute-start | bytes 786440 | tf_op jit(solution)/shard_map/ppermute | solution.py:285
  118.0 11.8 %collective-permute-start.4 = (f32[256,256]{1,0:T(8,128)S(1)}, f32[256,256]{1,0:T(8,128)S(1)}, u32[]{:S(2)}, u32[]{:S(2)}) collective-permute-start(f32[256,256]{1,0:T(8,128)S(1)} %collective-permute-done.3.refs_0_), channel_id=1, source_target_pairs={{0,4},{4,0},{8,12},{12,8},{1,5},{5,1},{9,13},{13,9},{2,6},{6,2},{1... | collective-permute-start | bytes 786440 | tf_op jit(solution)/shard_map/ppermute | solution.py:287
  120.4 10.2 %collective-permute-start.5 = (f32[256,256]{1,0:T(8,128)S(1)}, f32[256,256]{1,0:T(8,128)S(1)}, u32[]{:S(2)}, u32[]{:S(2)}) collective-permute-start(f32[256,256]{1,0:T(8,128)S(1)} %collective-permute-done.3.refs_0_), channel_id=1, source_target_pairs={{0,8},{4,12},{8,0},{12,4},{1,9},{5,13},{9,1},{13,5},{2,10},{6,14},... | collective-permute-start | bytes 786440 | tf_op jit(solution)/shard_map/ppermute | solution.py:287
  125.4 9.5 %collective-permute-start.6 = (f32[256,256]{1,0:T(8,128)S(1)}, f32[256,256]{1,0:T(8,128)S(1)}, u32[]{:S(2)}, u32[]{:S(2)}) collective-permute-start(f32[256,256]{1,0:T(8,128)S(1)} %collective-permute-done.3.refs_0_), channel_id=1, source_target_pairs={{0,12},{4,8},{8,4},{12,0},{1,13},{5,9},{9,5},{13,1},{2,14},{6,10},... | collective-permute-start | bytes 786440 | tf_op jit(solution)/shard_map/ppermute | solution.py:287

commit v5 on v4

--- a/solution.py
+++ b/solution.py
@@ -17,10 +17,10 @@
 CHUNK = 32
 
 
-def mirrored():
+def across():
     pairs = []
     for z in range(8):
-        far = 7 - z
+        far = z ^ 6
         pairs.append(((z // 4 * 2 + 1) * 4 + z % 4, (far // 4 * 2) * 4 + far % 4))
     return pairs
 
@@ -282,7 +282,7 @@
     )(state, gathered_sums(sums, mask))
     near = lax.ppermute(wave_out, "core", SWAP)
     y = lax.axis_index("y")
-    far = [lax.ppermute(lax.dynamic_slice_in_dim(wave_out, y * width, width), SEC + ("z1", "z0"), mirrored())]
+    far = [lax.ppermute(lax.dynamic_slice_in_dim(wave_out, y * width, width), SEC + ("z1", "z0"), across())]
     for k in range(1, sectors):
         far.append(lax.ppermute(far[0], ("core", "y"), [(i, i ^ k) for i in range(sectors)]))
     place = jnp.stack([lax.axis_index("core"), y]).astype(jnp.int32).reshape(1, 2)

time: 137 us -> 138 us (level)
  the two profiles are of different devices: /device:TPU:0 before, /device:TPU:32 now
where the time goes in v5:
time: 138 us
  blocking collectives  84.7 us (61%)
  waiting for transfers between devices  20.9 us (15%)
  starting transfers between devices  16.8 us (12%)
  Pallas kernels  14.7 us (11%)
    all_to_all x2, blocking collectives, gathered_sums(): lax.all_to_all(partial.reshape(ways, rows // ways, width), NEAR, 0, 0)  44.9 us
    all_to_all x2, blocking collectives, gathered_sums(): return lax.all_to_all(copies, NEAR, 0, 0).reshape(rows, width)  39.8 us
    ppermute x1, waiting for transfers between devices, shards(): lax.ppermute(lax.dynamic_slice_in_dim(wave_out, y * width, width), SEC +...  11.3 us
    ppermute x3, starting transfers between devices, shards(): lax.ppermute(far[0], ('core', 'y'), [(i, i ^ k) for i in range(sectors)])  10.4 us
    pallas_call x1, Pallas kernels, first_sums(): pl.pallas_call(first_kernel, in_specs=[hbm()] * 4, out_specs=[vmem()] * 3...  5.27 us
    ppermute x2, waiting for transfers between devices, gathered_sums(): lax.ppermute(piece, 'z1', SWAP)  5.19 us
    pallas_call x1, Pallas kernels, second_sums(): pl.pallas_call(second_kernel, in_specs=[vmem()] * 2 + [hbm()] * 2, out_sp...  5.13 us
    ppermute x2, starting transfers between devices, gathered_sums(): lax.ppermute(piece, 'z1', SWAP)  4.97 us
  transfers between devices with their start and end apart: 7, of which 5 were waited for; matrix products, arithmetic and copies ran while one was open for 0% of the time, Pallas kernels for 1%

profile of v5, /device:TPU:32, one launch (start us, length us, event | category | flops | bytes accessed | tf_op | source)
XLA Modules:
  0.0 138.2 jit_solution(4254562135587308584)
XLA Ops:
  0.6 5.3 %shard_map.59 = (f32[1024,256]{1,0:T(8,128)S(1)}, f32[1024,256]{1,0:T(8,128)S(1)}, f32[4,8,256]{2,1,0:T(8,128)S(1)}) custom-call(s32[1,4]{1,0:T(1,128)} %kept_hbm.1, f32[1024,256]{1,0:T(8,128)} %bitcast.21, bf16[8,4,256,256]{3,2,1,0:T(8,128)(2,1)} %bitcast.17, bf16[8,4,256,256]{3,2,1,0:T(8,128)(2,1)} %bitcast.19), custom_call_target="tpu_custom_call" | custom-call | flops 2147483648 | bytes 8388608 | tf_op jit(solution)/shard_map/pallas_call | solution.py:217
  5.9 24.6 %all_to_all.20 = f32[32,32,256]{2,1,0:T(8,128)S(1)} all-to-all(f32[32,32,256]{2,1,0:T(8,128)S(1)} %bitcast.16), channel_id=1, replica_groups=mesh['zh'=2,'core'=2,'z1'=2,'z0'=2,'y'=4,'x'=4] {'z0','y','x'}, dimensions={0} | all-to-all | bytes 2097152 | tf_op jit(solution)/shard_map/all_to_all | solution.py:255
  30.5 0.1 reduce_sum.18.here_ref
  30.6 3.4 %collective-permute-start = (f32[32,256]{1,0:T(8,128)S(1)}, f32[32,256]{1,0:T(8,128)S(1)}, u32[]{:S(2)}, u32[]{:S(2)}) collective-permute-start(f32[32,256]{1,0:T(8,128)S(1)} %reduce_sum.18.here_ref), channel_id=1, source_target_pairs={{0,32},{32,0},{1,33},{33,1},{2,34},{34,2},{3,35},{35,3},{4,36},{36... | collective-permute-start | bytes 98312 | tf_op jit(solution)/shard_map/ppermute | solution.py:263
  33.9 1.9 %collective-permute-done.there_ref = f32[32,256]{1,0:T(8,128)S(1)} collective-permute-done((f32[32,256]{1,0:T(8,128)S(1)}, f32[32,256]{1,0:T(8,128)S(1)}, u32[]{:S(2)}, u32[]{:S(2)}) %collective-permute-start) | collective-permute-done | bytes 32800 | tf_op jit(solution)/shard_map/ppermute | solution.py:263
  35.8 0.1 shard_map.60
  35.9 20.6 %all_to_all.21 = f32[32,32,256]{2,1,0:T(8,128)S(1)} all-to-all(f32[32,32,256]{2,1,0:T(8,128)S(1)} %shard_map.60), channel_id=1, replica_groups=mesh['zh'=2,'core'=2,'z1'=2,'z0'=2,'y'=4,'x'=4] {'z0','y','x'}, dimensions={0} | all-to-all | bytes 2097152 | tf_op jit(solution)/shard_map/all_to_all | solution.py:264
  56.5 5.1 %shard_map.61 = (f32[1024,256]{1,0:T(8,128)S(1)}, f32[1024,256]{1,0:T(8,128)S(1)}) custom-call(f32[1024,256]{1,0:T(8,128)S(1)} %get-tuple-element.11.old_ref, f32[1024,256]{1,0:T(8,128)S(1)} %bitcast.13, bf16[8,4,256,256]{3,2,1,0:T(8,128)(2,1)} %bitcast.18, bf16[8,4,256,256]{3,2,1,0:T(8,128)(2,1)} %bitcast.20), custom_call_target="tpu_custom_call" | custom-call | flops 2147483648 | bytes 8388608 | tf_op jit(solution)/shard_map/pallas_call | solution.py:237
  61.6 20.4 %all_to_all.22 = f32[32,32,256]{2,1,0:T(8,128)S(1)} all-to-all(f32[32,32,256]{2,1,0:T(8,128)S(1)} %bitcast.15), channel_id=1, replica_groups=mesh['zh'=2,'core'=2,'z1'=2,'z0'=2,'y'=4,'x'=4] {'z0','y','x'}, dimensions={0} | all-to-all | bytes 2097152 | tf_op jit(solution)/shard_map/all_to_all | solution.py:255
  82.0 0.1 reduce_sum.19.here_ref
  82.1 1.6 %collective-permute-start.1 = (f32[32,256]{1,0:T(8,128)S(1)}, f32[32,256]{1,0:T(8,128)S(1)}, u32[]{:S(2)}, u32[]{:S(2)}) collective-permute-start(f32[32,256]{1,0:T(8,128)S(1)} %reduce_sum.19.here_ref), channel_id=1, source_target_pairs={{0,32},{32,0},{1,33},{33,1},{2,34},{34,2},{3,35},{35,3},{4,36},{36... | collective-permute-start | bytes 98312 | tf_op jit(solution)/shard_map/ppermute | solution.py:263
  83.7 3.3 %collective-permute-done.1.there_ref = f32[32,256]{1,0:T(8,128)S(1)} collective-permute-done((f32[32,256]{1,0:T(8,128)S(1)}, f32[32,256]{1,0:T(8,128)S(1)}, u32[]{:S(2)}, u32[]{:S(2)}) %collective-permute-start.1) | collective-permute-done | bytes 32800 | tf_op jit(solution)/shard_map/ppermute | solution.py:263
  87.0 0.1 shard_map.62
  87.1 19.2 %all_to_all.23 = f32[32,32,256]{2,1,0:T(8,128)S(1)} all-to-all(f32[32,32,256]{2,1,0:T(8,128)S(1)} %shard_map.62), channel_id=1, replica_groups=mesh['zh'=2,'core'=2,'z1'=2,'z0'=2,'y'=4,'x'=4] {'z0','y','x'}, dimensions={0} | all-to-all | bytes 2097152 | tf_op jit(solution)/shard_map/all_to_all | solution.py:264
  106.3 0.9 shard_map.63.wave_ref
  107.2 0.1 collective-permute-start.2
  107.3 1.3 collective-permute-start.3
  108.6 11.3 %collective-permute-done.3.refs_0_ = f32[256,256]{1,0:T(8,128)S(1)} collective-permute-done((f32[256,256]{1,0:T(8,128)S(1)}, f32[256,256]{1,0:T(8,128)S(1)}, u32[]{:S(2)}, u32[]{:S(2)}) %collective-permute-start.3) | collective-permute-done | bytes 262176 | tf_op jit(solution)/shard_map/ppermute | solution.py:285
  119.9 2.7 %collective-permute-start.4 = (f32[256,256]{1,0:T(8,128)S(1)}, f32[256,256]{1,0:T(8,128)S(1)}, u32[]{:S(2)}, u32[]{:S(2)}) collective-permute-start(f32[256,256]{1,0:T(8,128)S(1)} %collective-permute-done.3.refs_0_), channel_id=1, source_target_pairs={{0,4},{4,0},{8,12},{12,8},{1,5},{5,1},{9,13},{13,9},{2,6},{6,2},{1... | collective-permute-start | bytes 786440 | tf_op jit(solution)/shard_map/ppermute | solution.py:287
  122.6 4.1 %collective-permute-start.5 = (f32[256,256]{1,0:T(8,128)S(1)}, f32[256,256]{1,0:T(8,128)S(1)}, u32[]{:S(2)}, u32[]{:S(2)}) collective-permute-start(f32[256,256]{1,0:T(8,128)S(1)} %collective-permute-done.3.refs_0_), channel_id=1, source_target_pairs={{0,8},{4,12},{8,0},{12,4},{1,9},{5,13},{9,1},{13,5},{2,10},{6,14},... | collective-permute-start | bytes 786440 | tf_op jit(solution)/shard_map/ppermute | solution.py:287
  126.7 3.7 %collective-permute-start.6 = (f32[256,256]{1,0:T(8,128)S(1)}, f32[256,256]{1,0:T(8,128)S(1)}, u32[]{:S(2)}, u32[]{:S(2)}) collective-permute-start(f32[256,256]{1,0:T(8,128)S(1)} %collective-permute-done.3.refs_0_), channel_id=1, source_target_pairs={{0,12},{4,8},{8,4},{12,0},{1,13},{5,9},{9,5},{13,1},{2,14},{6,10},... | collective-permute-start | bytes 786440 | tf_op jit(solution)/shard_map/ppermute | solution.py:287
  130.4 0.1 add_bitcast_fusion.place_ref
  130.4 0.0 collective-permute-done.2.near_ref
  130.4 1.3 shard_map.64
  131.7 0.0 collective-permute-done.4.refs_1_
  131.7 0.6 collective-permute-done.5.refs_2_
  132.4 3.8 %collective-permute-done.6.refs_3_ = f32[256,256]{1,0:T(8,128)S(1)} collective-permute-done((f32[256,256]{1,0:T(8,128)S(1)}, f32[256,256]{1,0:T(8,128)S(1)}, u32[]{:S(2)}, u32[]{:S(2)}) %collective-permute-start.6) | collective-permute-done | bytes 262176 | tf_op jit(solution)/shard_map/ppermute | solution.py:287
  136.2 2.0 %shard_map.65 = f32[1024,256]{1,0:T(8,128)} custom-call(s32[1,2]{1,0:T(1,128)S(1)} %add_bitcast_fusion.place_ref, f32[1024,256]{1,0:T(8,128)S(1)} %get-tuple-element.17.product_ref, bf16[1024,256]{1,0:T(8,128)(2,1)S(1)} %get-tuple-element.18.high_ref, bf16[1024,256]{1,0:T(8,128)(2,1)S(1)} %get-tuple-element.19.low_ref, ...), custom_call_target="tpu_custom_call" | custom-call | flops 402653184 | bytes 4194304 | tf_op jit(solution)/shard_map/pallas_call | solution.py:298
  (1 shorter events, 0.0 us)
Async XLA Ops:
  30.6 5.3 %collective-permute-start = (f32[32,256]{1,0:T(8,128)S(1)}, f32[32,256]{1,0:T(8,128)S(1)}, u32[]{:S(2)}, u32[]{:S(2)}) collective-permute-start(f32[32,256]{1,0:T(8,128)S(1)} %reduce_sum.18.here_ref), channel_id=1, source_target_pairs={{0,32},{32,0},{1,33},{33,1},{2,34},{34,2},{3,35},{35,3},{4,36},{36... | collective-permute-start | bytes 98312 | tf_op jit(solution)/shard_map/ppermute | solution.py:263
  82.1 4.9 %collective-permute-start.1 = (f32[32,256]{1,0:T(8,128)S(1)}, f32[32,256]{1,0:T(8,128)S(1)}, u32[]{:S(2)}, u32[]{:S(2)}) collective-permute-start(f32[32,256]{1,0:T(8,128)S(1)} %reduce_sum.19.here_ref), channel_id=1, source_target_pairs={{0,32},{32,0},{1,33},{33,1},{2,34},{34,2},{3,35},{35,3},{4,36},{36... | collective-permute-start | bytes 98312 | tf_op jit(solution)/shard_map/ppermute | solution.py:263
  107.2 23.3 %collective-permute-start.2 = (f32[1024,256]{1,0:T(8,128)S(1)}, f32[1024,256]{1,0:T(8,128)S(1)}, u32[]{:S(2)}, u32[]{:S(2)}) collective-permute-start(f32[1024,256]{1,0:T(8,128)S(1)} %shard_map.63.wave_ref), channel_id=1, source_target_pairs={{0,64},{64,0},{1,65},{65,1},{2,66},{66,2},{3,67},{67,3},{4,68},{68... | collective-permute-start | bytes 3145736 | tf_op jit(solution)/shard_map/ppermute | solution.py:283
  107.3 12.6 %collective-permute-start.3 = (f32[256,256]{1,0:T(8,128)S(1)}, f32[256,256]{1,0:T(8,128)S(1)}, u32[]{:S(2)}, u32[]{:S(2)}) collective-permute-start(f32[256,256]{1,0:T(8,128)S(1)} %constant_dynamic-slice_fusion), channel_id=1, source_target_pairs={{64,160},{80,176},{96,128},{112,144},{192,32},{208,48},{224,0},{24... | collective-permute-start | bytes 786440 | tf_op jit(solution)/shard_map/ppermute | solution.py:285
  119.9 11.8 %collective-permute-start.4 = (f32[256,256]{1,0:T(8,128)S(1)}, f32[256,256]{1,0:T(8,128)S(1)}, u32[]{:S(2)}, u32[]{:S(2)}) collective-permute-start(f32[256,256]{1,0:T(8,128)S(1)} %collective-permute-done.3.refs_0_), channel_id=1, source_target_pairs={{0,4},{4,0},{8,12},{12,8},{1,5},{5,1},{9,13},{13,9},{2,6},{6,2},{1... | collective-permute-start | bytes 786440 | tf_op jit(solution)/shard_map/ppermute | solution.py:287
  122.6 9.8 %collective-permute-start.5 = (f32[256,256]{1,0:T(8,128)S(1)}, f32[256,256]{1,0:T(8,128)S(1)}, u32[]{:S(2)}, u32[]{:S(2)}) collective-permute-start(f32[256,256]{1,0:T(8,128)S(1)} %collective-permute-done.3.refs_0_), channel_id=1, source_target_pairs={{0,8},{4,12},{8,0},{12,4},{1,9},{5,13},{9,1},{13,5},{2,10},{6,14},... | collective-permute-start | bytes 786440 | tf_op jit(solution)/shard_map/ppermute | solution.py:287
  126.7 9.5 %collective-permute-start.6 = (f32[256,256]{1,0:T(8,128)S(1)}, f32[256,256]{1,0:T(8,128)S(1)}, u32[]{:S(2)}, u32[]{:S(2)}) collective-permute-start(f32[256,256]{1,0:T(8,128)S(1)} %collective-permute-done.3.refs_0_), channel_id=1, source_target_pairs={{0,12},{4,8},{8,4},{12,0},{1,13},{5,9},{9,5},{13,1},{2,14},{6,10},... | collective-permute-start | bytes 786440 | tf_op jit(solution)/shard_map/ppermute | solution.py:287

commit v6 on v4

--- a/solution.py
+++ b/solution.py
@@ -152,7 +152,14 @@
     return high, (block - high.astype(jnp.float32)).astype(jnp.bfloat16)
 
 
-def near_kernel(wave_ref, near_ref, wave_out, product_ref, high_ref, low_ref, sem):
+def far_product(rows, high_ref, low_ref, far):
+    far_high, far_low = halves(far)
+    total = jnp.dot(high_ref[rows, :], far_high, preferred_element_type=jnp.float32)
+    total += jnp.dot(high_ref[rows, :], far_low, preferred_element_type=jnp.float32)
+    return total + jnp.dot(low_ref[rows, :], far_high, preferred_element_type=jnp.float32)
+
+
+def near_kernel(place_ref, wave_ref, near_ref, far_ref, wave_out, product_ref, high_ref, low_ref, sem):
     leaving = pltpu.make_async_copy(wave_ref, wave_out, sem)
     leaving.start()
     rows, width = wave_ref.shape
@@ -163,27 +170,28 @@
         product_ref[part, :] = jnp.dot(
             wave, near_ref[part, :], precision=lax.Precision.HIGHEST, preferred_element_type=jnp.float32
         )
+    rows = pl.ds(pl.multiple_of(place_ref[0, 1] * width, width), width)
+    near = product_ref[rows, :]
+    far = far_product(rows, high_ref, low_ref, far_ref[...])
+    product_ref[rows, :] = (near + jnp.where(place_ref[0, 0] == 0, far, near)) / math.sqrt(width)
     leaving.wait()
 
 
 def bound_kernel(place_ref, product_ref, high_ref, low_ref, *refs):
-    sectors = len(refs) - 3
-    far_refs, (out_hbm, bound_ref, sems) = refs[:sectors], refs[sectors:]
+    sectors = len(refs) - 2
+    far_refs, (out_hbm, bound_ref, sems) = refs[: sectors - 1], refs[sectors - 1 :]
     width = product_ref.shape[1]
     even = place_ref[0, 0] == 0
     copies = []
     for k in range(sectors):
         rows = pl.ds(pl.multiple_of((place_ref[0, 1] ^ k) * width, width), width)
-        far_high, far_low = halves(far_refs[k][...])
-        near = product_ref[rows, :]
-        far = jnp.dot(high_ref[rows, :], far_high, preferred_element_type=jnp.float32)
-        far += jnp.dot(high_ref[rows, :], far_low, preferred_element_type=jnp.float32)
-        far += jnp.dot(low_ref[rows, :], far_high, preferred_element_type=jnp.float32)
-        bound_ref[rows, :] = (near + jnp.where(even, far, near)) / math.sqrt(width)
-        copies.append(pltpu.make_async_copy(bound_ref.at[rows], out_hbm.at[rows], sems.at[k]))
-        if k % 2:
-            copies[k - 1].start()
-            copies[k].start()
+        source = bound_ref if k else product_ref
+        if k:
+            near = product_ref[rows, :]
+            far = far_product(rows, high_ref, low_ref, far_refs[k - 1][...])
+            bound_ref[rows, :] = (near + jnp.where(even, far, near)) / math.sqrt(width)
+        copies.append(pltpu.make_async_copy(source.at[rows], out_hbm.at[rows], sems.at[k]))
+        copies[k].start()
     for copy in copies:
         copy.wait()
 
@@ -288,22 +296,22 @@
     place = jnp.stack([lax.axis_index("core"), y]).astype(jnp.int32).reshape(1, 2)
     wave_out, *products = pl.pallas_call(
         near_kernel,
-        in_specs=[vmem()] * 2,
+        in_specs=[smem()] + [vmem()] * 3,
         out_specs=[hbm()] + [vmem()] * 3,
         out_shape=[like, like] + [jax.ShapeDtypeStruct(wave.shape, jnp.bfloat16)] * 2,
         scratch_shapes=[pltpu.SemaphoreType.DMA],
         compiler_params=params(),
         cost_estimate=cost(12 * sectors * width**3, 16 * wave.size),
-    )(wave_out, near)
+    )(place, wave_out, near, far[0])
     bound = pl.pallas_call(
         bound_kernel,
-        in_specs=[smem()] + [vmem()] * (3 + sectors),
+        in_specs=[smem()] + [vmem()] * (2 + sectors),
         out_specs=hbm(),
         out_shape=like,
         scratch_shapes=[pltpu.VMEM(wave.shape, jnp.float32), pltpu.SemaphoreType.DMA((sectors,))],
         compiler_params=params(),
         cost_estimate=cost(6 * sectors * width**3, 16 * wave.size),
-    )(place, *products, *far)
+    )(place, *products, *far[1:])
     return (wave_out.reshape(wave_in.shape), bound.reshape(wave_in.shape))
 
 

time: 137 us -> 137 us (level)
  no operation moved by 1% of the time
where the time goes in v6:
time: 137 us
  blocking collectives  83.7 us (61%)
  waiting for transfers between devices  20.1 us (15%)
  starting transfers between devices  16.8 us (12%)
  Pallas kernels  15.2 us (11%)
    all_to_all x2, blocking collectives, gathered_sums(): lax.all_to_all(partial.reshape(ways, rows // ways, width), NEAR, 0, 0)  43.6 us
    all_to_all x2, blocking collectives, gathered_sums(): return lax.all_to_all(copies, NEAR, 0, 0).reshape(rows, width)  40.1 us
    ppermute x3, starting transfers between devices, shards(): lax.ppermute(far[0], ('core', 'y'), [(i, i ^ k) for i in range(sectors)])  10.4 us
    ppermute x1, waiting for transfers between devices, shards(): lax.ppermute(lax.dynamic_slice_in_dim(wave_out, y * width, width), SEC +...  10.4 us
    pallas_call x1, Pallas kernels, first_sums(): pl.pallas_call(first_kernel, in_specs=[hbm()] * 4, out_specs=[vmem()] * 3...  5.27 us
    ppermute x2, waiting for transfers between devices, gathered_sums(): lax.ppermute(piece, 'z1', SWAP)  5.15 us
    pallas_call x1, Pallas kernels, second_sums(): pl.pallas_call(second_kernel, in_specs=[vmem()] * 2 + [hbm()] * 2, out_sp...  5.13 us
    ppermute x2, starting transfers between devices, gathered_sums(): lax.ppermute(piece, 'z1', SWAP)  5 us
  transfers between devices with their start and end apart: 7, of which 5 were waited for; matrix products, arithmetic and copies ran while one was open for 0% of the time, Pallas kernels for 1%

profile of v6, /device:TPU:0, one launch (start us, length us, event | category | flops | bytes accessed | tf_op | source)
XLA Modules:
  0.0 136.8 jit_solution(9698851506110133551)
XLA Ops:
  0.6 5.3 %shard_map.59 = (f32[1024,256]{1,0:T(8,128)S(1)}, f32[1024,256]{1,0:T(8,128)S(1)}, f32[4,8,256]{2,1,0:T(8,128)S(1)}) custom-call(s32[1,4]{1,0:T(1,128)} %kept_hbm.1, f32[1024,256]{1,0:T(8,128)} %bitcast.21, bf16[8,4,256,256]{3,2,1,0:T(8,128)(2,1)} %bitcast.17, bf16[8,4,256,256]{3,2,1,0:T(8,128)(2,1)} %bitcast.19), custom_call_target="tpu_custom_call" | custom-call | flops 2147483648 | bytes 8388608 | tf_op jit(solution)/shard_map/pallas_call | solution.py:225
  5.9 23.3 %all_to_all.20 = f32[32,32,256]{2,1,0:T(8,128)S(1)} all-to-all(f32[32,32,256]{2,1,0:T(8,128)S(1)} %bitcast.16), channel_id=1, replica_groups=mesh['zh'=2,'core'=2,'z1'=2,'z0'=2,'y'=4,'x'=4] {'z0','y','x'}, dimensions={0} | all-to-all | bytes 2097152 | tf_op jit(solution)/shard_map/all_to_all | solution.py:263
  29.2 0.1 reduce_sum.18.here_ref
  29.2 3.4 %collective-permute-start = (f32[32,256]{1,0:T(8,128)S(1)}, f32[32,256]{1,0:T(8,128)S(1)}, u32[]{:S(2)}, u32[]{:S(2)}) collective-permute-start(f32[32,256]{1,0:T(8,128)S(1)} %reduce_sum.18.here_ref), channel_id=1, source_target_pairs={{0,32},{32,0},{1,33},{33,1},{2,34},{34,2},{3,35},{35,3},{4,36},{36... | collective-permute-start | bytes 98312 | tf_op jit(solution)/shard_map/ppermute | solution.py:271
  32.6 1.9 %collective-permute-done.there_ref = f32[32,256]{1,0:T(8,128)S(1)} collective-permute-done((f32[32,256]{1,0:T(8,128)S(1)}, f32[32,256]{1,0:T(8,128)S(1)}, u32[]{:S(2)}, u32[]{:S(2)}) %collective-permute-start) | collective-permute-done | bytes 32800 | tf_op jit(solution)/shard_map/ppermute | solution.py:271
  34.5 0.1 shard_map.60
  34.6 20.8 %all_to_all.21 = f32[32,32,256]{2,1,0:T(8,128)S(1)} all-to-all(f32[32,32,256]{2,1,0:T(8,128)S(1)} %shard_map.60), channel_id=1, replica_groups=mesh['zh'=2,'core'=2,'z1'=2,'z0'=2,'y'=4,'x'=4] {'z0','y','x'}, dimensions={0} | all-to-all | bytes 2097152 | tf_op jit(solution)/shard_map/all_to_all | solution.py:272
  55.4 5.1 %shard_map.61 = (f32[1024,256]{1,0:T(8,128)S(1)}, f32[1024,256]{1,0:T(8,128)S(1)}) custom-call(f32[1024,256]{1,0:T(8,128)S(1)} %get-tuple-element.11.old_ref, f32[1024,256]{1,0:T(8,128)S(1)} %bitcast.13, bf16[8,4,256,256]{3,2,1,0:T(8,128)(2,1)} %bitcast.18, bf16[8,4,256,256]{3,2,1,0:T(8,128)(2,1)} %bitcast.20), custom_call_target="tpu_custom_call" | custom-call | flops 2147483648 | bytes 8388608 | tf_op jit(solution)/shard_map/pallas_call | solution.py:245
  60.6 20.4 %all_to_all.22 = f32[32,32,256]{2,1,0:T(8,128)S(1)} all-to-all(f32[32,32,256]{2,1,0:T(8,128)S(1)} %bitcast.15), channel_id=1, replica_groups=mesh['zh'=2,'core'=2,'z1'=2,'z0'=2,'y'=4,'x'=4] {'z0','y','x'}, dimensions={0} | all-to-all | bytes 2097152 | tf_op jit(solution)/shard_map/all_to_all | solution.py:263
  80.9 0.1 reduce_sum.19.here_ref
  81.0 1.6 %collective-permute-start.1 = (f32[32,256]{1,0:T(8,128)S(1)}, f32[32,256]{1,0:T(8,128)S(1)}, u32[]{:S(2)}, u32[]{:S(2)}) collective-permute-start(f32[32,256]{1,0:T(8,128)S(1)} %reduce_sum.19.here_ref), channel_id=1, source_target_pairs={{0,32},{32,0},{1,33},{33,1},{2,34},{34,2},{3,35},{35,3},{4,36},{36... | collective-permute-start | bytes 98312 | tf_op jit(solution)/shard_map/ppermute | solution.py:271
  82.6 3.3 %collective-permute-done.1.there_ref = f32[32,256]{1,0:T(8,128)S(1)} collective-permute-done((f32[32,256]{1,0:T(8,128)S(1)}, f32[32,256]{1,0:T(8,128)S(1)}, u32[]{:S(2)}, u32[]{:S(2)}) %collective-permute-start.1) | collective-permute-done | bytes 32800 | tf_op jit(solution)/shard_map/ppermute | solution.py:271
  85.9 0.1 shard_map.62
  86.0 19.3 %all_to_all.23 = f32[32,32,256]{2,1,0:T(8,128)S(1)} all-to-all(f32[32,32,256]{2,1,0:T(8,128)S(1)} %shard_map.62), channel_id=1, replica_groups=mesh['zh'=2,'core'=2,'z1'=2,'z0'=2,'y'=4,'x'=4] {'z0','y','x'}, dimensions={0} | all-to-all | bytes 2097152 | tf_op jit(solution)/shard_map/all_to_all | solution.py:272
  105.3 0.9 shard_map.63.wave_ref
  106.1 0.1 collective-permute-start.2
  106.3 1.3 collective-permute-start.3
  107.6 10.4 %collective-permute-done.3.far_ref = f32[256,256]{1,0:T(8,128)S(1)} collective-permute-done((f32[256,256]{1,0:T(8,128)S(1)}, f32[256,256]{1,0:T(8,128)S(1)}, u32[]{:S(2)}, u32[]{:S(2)}) %collective-permute-start.3) | collective-permute-done | bytes 262176 | tf_op jit(solution)/shard_map/ppermute | solution.py:293
  118.0 2.4 %collective-permute-start.4 = (f32[256,256]{1,0:T(8,128)S(1)}, f32[256,256]{1,0:T(8,128)S(1)}, u32[]{:S(2)}, u32[]{:S(2)}) collective-permute-start(f32[256,256]{1,0:T(8,128)S(1)} %collective-permute-done.3.far_ref), channel_id=1, source_target_pairs={{0,4},{4,0},{8,12},{12,8},{1,5},{5,1},{9,13},{13,9},{2,6},{6,2},{1... | collective-permute-start | bytes 786440 | tf_op jit(solution)/shard_map/ppermute | solution.py:295
  120.4 5.0 %collective-permute-start.5 = (f32[256,256]{1,0:T(8,128)S(1)}, f32[256,256]{1,0:T(8,128)S(1)}, u32[]{:S(2)}, u32[]{:S(2)}) collective-permute-start(f32[256,256]{1,0:T(8,128)S(1)} %collective-permute-done.3.far_ref), channel_id=1, source_target_pairs={{0,8},{4,12},{8,0},{12,4},{1,9},{5,13},{9,1},{13,5},{2,10},{6,14},... | collective-permute-start | bytes 786440 | tf_op jit(solution)/shard_map/ppermute | solution.py:295
  125.4 3.0 %collective-permute-start.6 = (f32[256,256]{1,0:T(8,128)S(1)}, f32[256,256]{1,0:T(8,128)S(1)}, u32[]{:S(2)}, u32[]{:S(2)}) collective-permute-start(f32[256,256]{1,0:T(8,128)S(1)} %collective-permute-done.3.far_ref), channel_id=1, source_target_pairs={{0,12},{4,8},{8,4},{12,0},{1,13},{5,9},{9,5},{13,1},{2,14},{6,10},... | collective-permute-start | bytes 786440 | tf_op jit(solution)/shard_map/ppermute | solution.py:295
  128.4 0.1 add_bitcast_fusion.place_ref
  128.5 0.0 collective-permute-done.2.near_ref
  128.5 1.8 %shard_map.64 = (f32[1024,256]{1,0:T(8,128)}, f32[1024,256]{1,0:T(8,128)S(1)}, bf16[1024,256]{1,0:T(8,128)(2,1)S(1)}, bf16[1024,256]{1,0:T(8,128)(2,1)S(1)}) custom-call(s32[1,2]{1,0:T(1,128)S(1)} %add_bitcast_fusion.place_ref, f32[1024,256]{1,0:T(8,128)S(1)} %shard_map.63.wave_ref, f32[1024,256]{1,0:T(8,128)S(1)} %collective-permute-done.2.near_ref, ...), custom_call_target="tpu_custom_call" | custom-call | flops 805306368 | bytes 4194304 | tf_op jit(solution)/shard_map/pallas_call | solution.py:297
  130.4 0.0 collective-permute-done.4.refs_0_
  130.4 0.3 collective-permute-done.5.refs_1_
  130.7 4.3 %collective-permute-done.6.refs_2_ = f32[256,256]{1,0:T(8,128)S(1)} collective-permute-done((f32[256,256]{1,0:T(8,128)S(1)}, f32[256,256]{1,0:T(8,128)S(1)}, u32[]{:S(2)}, u32[]{:S(2)}) %collective-permute-start.6) | collective-permute-done | bytes 262176 | tf_op jit(solution)/shard_map/ppermute | solution.py:295
  134.9 1.9 %shard_map.65 = f32[1024,256]{1,0:T(8,128)} custom-call(s32[1,2]{1,0:T(1,128)S(1)} %add_bitcast_fusion.place_ref, f32[1024,256]{1,0:T(8,128)S(1)} %get-tuple-element.17.product_ref, bf16[1024,256]{1,0:T(8,128)(2,1)S(1)} %get-tuple-element.18.high_ref, bf16[1024,256]{1,0:T(8,128)(2,1)S(1)} %get-tuple-element.19.low_ref, ...), custom_call_target="tpu_custom_call" | custom-call | flops 402653184 | bytes 4194304 | tf_op jit(solution)/shard_map/pallas_call | solution.py:306
  (1 shorter events, 0.0 us)
Async XLA Ops:
  29.2 5.3 %collective-permute-start = (f32[32,256]{1,0:T(8,128)S(1)}, f32[32,256]{1,0:T(8,128)S(1)}, u32[]{:S(2)}, u32[]{:S(2)}) collective-permute-start(f32[32,256]{1,0:T(8,128)S(1)} %reduce_sum.18.here_ref), channel_id=1, source_target_pairs={{0,32},{32,0},{1,33},{33,1},{2,34},{34,2},{3,35},{35,3},{4,36},{36... | collective-permute-start | bytes 98312 | tf_op jit(solution)/shard_map/ppermute | solution.py:271
  81.0 4.9 %collective-permute-start.1 = (f32[32,256]{1,0:T(8,128)S(1)}, f32[32,256]{1,0:T(8,128)S(1)}, u32[]{:S(2)}, u32[]{:S(2)}) collective-permute-start(f32[32,256]{1,0:T(8,128)S(1)} %reduce_sum.19.here_ref), channel_id=1, source_target_pairs={{0,32},{32,0},{1,33},{33,1},{2,34},{34,2},{3,35},{35,3},{4,36},{36... | collective-permute-start | bytes 98312 | tf_op jit(solution)/shard_map/ppermute | solution.py:271
  106.1 22.4 %collective-permute-start.2 = (f32[1024,256]{1,0:T(8,128)S(1)}, f32[1024,256]{1,0:T(8,128)S(1)}, u32[]{:S(2)}, u32[]{:S(2)}) collective-permute-start(f32[1024,256]{1,0:T(8,128)S(1)} %shard_map.63.wave_ref), channel_id=1, source_target_pairs={{0,64},{64,0},{1,65},{65,1},{2,66},{66,2},{3,67},{67,3},{4,68},{68... | collective-permute-start | bytes 3145736 | tf_op jit(solution)/shard_map/ppermute | solution.py:291
  106.3 11.7 %collective-permute-start.3 = (f32[256,256]{1,0:T(8,128)S(1)}, f32[256,256]{1,0:T(8,128)S(1)}, u32[]{:S(2)}, u32[]{:S(2)}) collective-permute-start(f32[256,256]{1,0:T(8,128)S(1)} %constant_dynamic-slice_fusion), channel_id=1, source_target_pairs={{64,176},{80,160},{96,144},{112,128},{192,48},{208,32},{224,16},{2... | collective-permute-start | bytes 786440 | tf_op jit(solution)/shard_map/ppermute | solution.py:293
  118.0 12.4 %collective-permute-start.4 = (f32[256,256]{1,0:T(8,128)S(1)}, f32[256,256]{1,0:T(8,128)S(1)}, u32[]{:S(2)}, u32[]{:S(2)}) collective-permute-start(f32[256,256]{1,0:T(8,128)S(1)} %collective-permute-done.3.far_ref), channel_id=1, source_target_pairs={{0,4},{4,0},{8,12},{12,8},{1,5},{5,1},{9,13},{13,9},{2,6},{6,2},{1... | collective-permute-start | bytes 786440 | tf_op jit(solution)/shard_map/ppermute | solution.py:295
  120.4 10.2 %collective-permute-start.5 = (f32[256,256]{1,0:T(8,128)S(1)}, f32[256,256]{1,0:T(8,128)S(1)}, u32[]{:S(2)}, u32[]{:S(2)}) collective-permute-start(f32[256,256]{1,0:T(8,128)S(1)} %collective-permute-done.3.far_ref), channel_id=1, source_target_pairs={{0,8},{4,12},{8,0},{12,4},{1,9},{5,13},{9,1},{13,5},{2,10},{6,14},... | collective-permute-start | bytes 786440 | tf_op jit(solution)/shard_map/ppermute | solution.py:295
  125.4 9.5 %collective-permute-start.6 = (f32[256,256]{1,0:T(8,128)S(1)}, f32[256,256]{1,0:T(8,128)S(1)}, u32[]{:S(2)}, u32[]{:S(2)}) collective-permute-start(f32[256,256]{1,0:T(8,128)S(1)} %collective-permute-done.3.far_ref), channel_id=1, source_target_pairs={{0,12},{4,8},{8,4},{12,0},{1,13},{5,9},{9,5},{13,1},{2,14},{6,10},... | collective-permute-start | bytes 786440 | tf_op jit(solution)/shard_map/ppermute | solution.py:295
